TPU v7x, 32 devices: a whole 2x2x4 slice. The times are simulated.
32 devices in a mesh: fsdp: 32 (over z, y, x, core).
Axes of the slice: x: 2, y: 2, z: 4, core: 2. Of those that a mesh axis runs over, the one named last changes fastest.
Arguments:
- tokens: bfloat16 [32768, 1024], P('fsdp'), may hold values from -6 to 6
- lengths: int32 [64], P('fsdp'), may hold values from 128 to 512, as said below
- cotangent: bfloat16 [32768, 1024], P('fsdp'), may hold values from -6 to 6
- query_weight: bfloat16 [1024, 1024], P('fsdp'), may hold values from -0.1875 to 0.1875
- query_bias: bfloat16 [1024], P('fsdp'), may hold values from -3 to 3
- key_weight: bfloat16 [1024, 1024], P('fsdp'), may hold values from -0.1875 to 0.1875
- value_weight: bfloat16 [1024, 1024], P('fsdp'), may hold values from -0.1875 to 0.1875
- value_bias: bfloat16 [1024], P('fsdp'), may hold values from -3 to 3
- attn_weight: bfloat16 [1024, 1024], P('fsdp'), may hold values from -1.5 to 1.5
- attn_bias: bfloat16 [1024], P('fsdp'), may hold values from -3 to 3
- first_gain: bfloat16 [1024], P('fsdp'), may hold values from 0.5 to 1.5
- first_shift: bfloat16 [1024], P('fsdp'), may hold values from -3 to 3
- inner_weight: bfloat16 [1024, 4096], P('fsdp'), may hold values from -0.1875 to 0.1875
- inner_bias: bfloat16 [4096], P('fsdp'), may hold values from -3 to 3
- outer_weight: bfloat16 [4096, 1024], P('fsdp'), may hold values from -0.09375 to 0.09375
- outer_bias: bfloat16 [1024], P('fsdp'), may hold values from -3 to 3
- second_gain: bfloat16 [1024], P('fsdp'), may hold values from 0.5 to 1.5
- second_shift: bfloat16 [1024], P('fsdp'), may hold values from -3 to 3
Outputs:
- output: bfloat16 [32768, 1024], P('fsdp')
- input_grad: bfloat16 [32768, 1024], P('fsdp')
- query_wgrad: float32 [1024, 1024], P('fsdp')
- query_bgrad: float32 [1024], P('fsdp')
- key_wgrad: float32 [1024, 1024], P('fsdp')
- value_wgrad: float32 [1024, 1024], P('fsdp')
- value_bgrad: float32 [1024], P('fsdp')
- attn_wgrad: float32 [1024, 1024], P('fsdp')
- attn_bgrad: float32 [1024], P('fsdp')
- first_ggrad: float32 [1024], P('fsdp')
- first_sgrad: float32 [1024], P('fsdp')
- inner_wgrad: float32 [1024, 4096], P('fsdp')
- inner_bgrad: float32 [4096], P('fsdp')
- outer_wgrad: float32 [4096, 1024], P('fsdp')
- outer_bgrad: float32 [1024], P('fsdp')
- second_ggrad: float32 [1024], P('fsdp')
- second_sgrad: float32 [1024], P('fsdp')
Inputs may be any that keep to these rules, and one draw needn't show every extreme that they name: The first lengths[s] slots of sequence s are valid; some sequence has exactly 512 valid slots and some has exactly 128.
All inputs are finite; a program needn't handle non-finite values.
Results may differ from a plain program's by a relative error of at most 0.014.
Values may be sent and summed in bfloat16 or wider, within the bound.
No kernel may reach another device: no remote copies, remote signals or barrier semaphores. Data moves between devices by JAX's collectives and lax.ppermute only.
A program may use at most 256 MiB of HBM per device.

v0:
```python
from functools import partial

import jax
import jax.numpy as jnp
from jax import lax
from jax.sharding import PartitionSpec as P

HEADS = 16
DHEAD = 64


EPSILON = 1e-05
MASKED = -1e30


def normalize(rows):
    centre = jnp.mean(rows, axis=-1, keepdims=True)
    centred = rows - centre
    factor = lax.rsqrt(jnp.mean(centred * centred, axis=-1, keepdims=True) + EPSILON)
    return (centred * factor, factor)


def norm_back(grad, normed, factor):
    mean_one = jnp.mean(grad, axis=-1, keepdims=True)
    mean_two = jnp.mean(grad * normed, axis=-1, keepdims=True)
    return factor * (grad - mean_one - normed * mean_two)


def across_rows(left, right):
    return lax.dot_general(
        left, right, (((0,), (0,)), ((), ())), preferred_element_type=jnp.float32
    )


def times_transpose(left, right):
    return lax.dot_general(
        left, right, (((1,), (1,)), ((), ())), preferred_element_type=jnp.float32
    )


def project(rows, matrix, bias):
    return jnp.dot(rows, matrix, preferred_element_type=jnp.float32) + bias.astype(jnp.float32)


def scores_of(query, keys, length):
    raw = jnp.einsum("qhd,khd->hqk", query, keys, preferred_element_type=jnp.float32) * DHEAD ** (
        -0.5
    )
    places = lax.broadcasted_iota(jnp.int32, raw.shape, 2)
    return jnp.where(places < length, raw, MASKED)


def attend(inputs):
    query, keys, values, length = inputs
    scores = scores_of(query, keys, length)
    top = jnp.max(scores, axis=-1, keepdims=True)
    expo = jnp.exp(scores - top)
    total = jnp.sum(expo, axis=-1, keepdims=True)
    probs_low = (expo / total).astype(jnp.bfloat16)
    mixed = jnp.einsum("hqk,khd->qhd", probs_low, values, preferred_element_type=jnp.float32)
    return (mixed, (top + jnp.log(total))[..., 0])


def attend_back(inputs):
    query, keys, values, length, grad_mixed, logsum = inputs
    scores = scores_of(query, keys, length)
    probs = jnp.exp(scores - logsum[..., None])
    probs_low = probs.astype(jnp.bfloat16)
    value_step = jnp.einsum(
        "hqk,qhd->khd", probs_low, grad_mixed, preferred_element_type=jnp.float32
    )
    grad_probs = jnp.einsum("qhd,khd->hqk", grad_mixed, values, preferred_element_type=jnp.float32)
    inner = jnp.sum(grad_probs * probs, axis=-1, keepdims=True)
    grad_scores = (probs * (grad_probs - inner)).astype(jnp.bfloat16)
    query_step = jnp.einsum(
        "hqk,khd->qhd", grad_scores, keys, preferred_element_type=jnp.float32
    ) * DHEAD ** (-0.5)
    key_step = jnp.einsum(
        "hqk,qhd->khd", grad_scores, query, preferred_element_type=jnp.float32
    ) * DHEAD ** (-0.5)
    return (
        query_step.astype(jnp.bfloat16),
        key_step.astype(jnp.bfloat16),
        value_step.astype(jnp.bfloat16),
    )


def per_device(
    tokens,
    lengths,
    cotangent,
    query_weight,
    query_bias,
    key_weight,
    value_weight,
    value_bias,
    attn_weight,
    attn_bias,
    first_gain,
    first_shift,
    inner_weight,
    inner_bias,
    outer_weight,
    outer_bias,
    second_gain,
    second_shift,
):
    seqs = lengths.shape[0]
    rows, width = tokens.shape
    span = rows // seqs
    shape = (seqs, span, HEADS, width // HEADS)
    gathered = (
        lax.all_gather(query_weight, "fsdp", axis=0, tiled=True),
        lax.all_gather(query_bias, "fsdp", axis=0, tiled=True),
        lax.all_gather(key_weight, "fsdp", axis=0, tiled=True),
        lax.all_gather(value_weight, "fsdp", axis=0, tiled=True),
        lax.all_gather(value_bias, "fsdp", axis=0, tiled=True),
        lax.all_gather(attn_weight, "fsdp", axis=0, tiled=True),
        lax.all_gather(attn_bias, "fsdp", axis=0, tiled=True),
        lax.all_gather(first_gain, "fsdp", axis=0, tiled=True),
        lax.all_gather(first_shift, "fsdp", axis=0, tiled=True),
        lax.all_gather(inner_weight, "fsdp", axis=0, tiled=True),
        lax.all_gather(inner_bias, "fsdp", axis=0, tiled=True),
        lax.all_gather(outer_weight, "fsdp", axis=0, tiled=True),
        lax.all_gather(outer_bias, "fsdp", axis=0, tiled=True),
        lax.all_gather(second_gain, "fsdp", axis=0, tiled=True),
        lax.all_gather(second_shift, "fsdp", axis=0, tiled=True),
    )
    (
        query_full,
        qbias_full,
        key_full,
        value_full,
        vbias_full,
        attn_full,
        abias_full,
        gain_first,
        shift_first,
        inner_full,
        ibias_full,
        outer_full,
        obias_full,
        gain_second,
        shift_second,
    ) = gathered
    query = project(tokens, query_full, qbias_full).astype(jnp.bfloat16)
    keys = jnp.dot(tokens, key_full, preferred_element_type=jnp.float32).astype(jnp.bfloat16)
    values = project(tokens, value_full, vbias_full).astype(jnp.bfloat16)
    mixed, logsum = lax.map(
        attend, (query.reshape(shape), keys.reshape(shape), values.reshape(shape), lengths)
    )
    mixed_low = mixed.reshape(rows, width).astype(jnp.bfloat16)
    first_sum = tokens.astype(jnp.float32) + project(mixed_low, attn_full, abias_full)
    first_normed, first_factor = normalize(first_sum)
    middle = first_normed * gain_first.astype(jnp.float32) + shift_first.astype(jnp.float32)
    middle_low = middle.astype(jnp.bfloat16)
    hidden = project(middle_low, inner_full, ibias_full)
    active_low = jax.nn.gelu(hidden, approximate=False).astype(jnp.bfloat16)
    second_sum = middle + project(active_low, outer_full, obias_full)
    second_normed, second_factor = normalize(second_sum)
    output = (
        second_normed * gain_second.astype(jnp.float32) + shift_second.astype(jnp.float32)
    ).astype(jnp.bfloat16)
    regathered = (
        lax.all_gather(query_weight, "fsdp", axis=0, tiled=True),
        lax.all_gather(query_bias, "fsdp", axis=0, tiled=True),
        lax.all_gather(key_weight, "fsdp", axis=0, tiled=True),
        lax.all_gather(value_weight, "fsdp", axis=0, tiled=True),
        lax.all_gather(value_bias, "fsdp", axis=0, tiled=True),
        lax.all_gather(attn_weight, "fsdp", axis=0, tiled=True),
        lax.all_gather(attn_bias, "fsdp", axis=0, tiled=True),
        lax.all_gather(first_gain, "fsdp", axis=0, tiled=True),
        lax.all_gather(first_shift, "fsdp", axis=0, tiled=True),
        lax.all_gather(inner_weight, "fsdp", axis=0, tiled=True),
        lax.all_gather(inner_bias, "fsdp", axis=0, tiled=True),
        lax.all_gather(outer_weight, "fsdp", axis=0, tiled=True),
        lax.all_gather(outer_bias, "fsdp", axis=0, tiled=True),
        lax.all_gather(second_gain, "fsdp", axis=0, tiled=True),
        lax.all_gather(second_shift, "fsdp", axis=0, tiled=True),
    )
    (
        query_full,
        qbias_full,
        key_full,
        value_full,
        vbias_full,
        attn_full,
        abias_full,
        gain_first,
        shift_first,
        inner_full,
        ibias_full,
        outer_full,
        obias_full,
        gain_second,
        shift_second,
    ) = regathered
    places = lax.broadcasted_iota(jnp.int32, (seqs, span), 1)
    valid = (places < lengths[:, None]).reshape(rows, 1)
    grad_out = jnp.where(valid, cotangent.astype(jnp.float32), 0.0)
    second_ggrad = jnp.sum(grad_out * second_normed, axis=0)
    second_sgrad = jnp.sum(grad_out, axis=0)
    grad_second = norm_back(
        grad_out * gain_second.astype(jnp.float32), second_normed, second_factor
    )
    grad_branch = grad_second.astype(jnp.bfloat16)
    outer_bgrad = jnp.sum(grad_branch.astype(jnp.float32), axis=0)
    outer_wgrad = across_rows(active_low, grad_branch)
    grad_active = times_transpose(grad_branch, outer_full)
    gelu_pull = jax.vjp(partial(jax.nn.gelu, approximate=False), hidden)[1]
    grad_hidden = gelu_pull(grad_active)[0].astype(jnp.bfloat16)
    inner_bgrad = jnp.sum(grad_hidden.astype(jnp.float32), axis=0)
    inner_wgrad = across_rows(middle_low, grad_hidden)
    grad_middle = grad_second + times_transpose(grad_hidden, inner_full)
    first_ggrad = jnp.sum(grad_middle * first_normed, axis=0)
    first_sgrad = jnp.sum(grad_middle, axis=0)
    grad_first = norm_back(grad_middle * gain_first.astype(jnp.float32), first_normed, first_factor)
    grad_proj = grad_first.astype(jnp.bfloat16)
    attn_bgrad = jnp.sum(grad_proj.astype(jnp.float32), axis=0)
    attn_wgrad = across_rows(mixed_low, grad_proj)
    grad_mixed = times_transpose(grad_proj, attn_full).astype(jnp.bfloat16)
    query_step, key_step, value_step = lax.map(
        attend_back,
        (
            query.reshape(shape),
            keys.reshape(shape),
            values.reshape(shape),
            lengths,
            grad_mixed.reshape(shape),
            logsum,
        ),
    )
    query_step = query_step.reshape(rows, width)
    key_step = key_step.reshape(rows, width)
    value_step = value_step.reshape(rows, width)
    query_bgrad = jnp.sum(query_step.astype(jnp.float32), axis=0)
    value_bgrad = jnp.sum(value_step.astype(jnp.float32), axis=0)
    query_wgrad = across_rows(tokens, query_step)
    key_wgrad = across_rows(tokens, key_step)
    value_wgrad = across_rows(tokens, value_step)
    input_sum = grad_first + times_transpose(query_step, query_full)
    input_sum = (
        input_sum + times_transpose(key_step, key_full) + times_transpose(value_step, value_full)
    )
    input_grad = input_sum.astype(jnp.bfloat16)
    (
        query_wgrad,
        query_bgrad,
        key_wgrad,
        value_wgrad,
        value_bgrad,
        attn_wgrad,
        attn_bgrad,
        first_ggrad,
        first_sgrad,
        inner_wgrad,
        inner_bgrad,
        outer_wgrad,
        outer_bgrad,
        second_ggrad,
        second_sgrad,
    ) = (
        lax.psum_scatter(query_wgrad, "fsdp", scatter_dimension=0, tiled=True),
        lax.psum_scatter(query_bgrad, "fsdp", scatter_dimension=0, tiled=True),
        lax.psum_scatter(key_wgrad, "fsdp", scatter_dimension=0, tiled=True),
        lax.psum_scatter(value_wgrad, "fsdp", scatter_dimension=0, tiled=True),
        lax.psum_scatter(value_bgrad, "fsdp", scatter_dimension=0, tiled=True),
        lax.psum_scatter(attn_wgrad, "fsdp", scatter_dimension=0, tiled=True),
        lax.psum_scatter(attn_bgrad, "fsdp", scatter_dimension=0, tiled=True),
        lax.psum_scatter(first_ggrad, "fsdp", scatter_dimension=0, tiled=True),
        lax.psum_scatter(first_sgrad, "fsdp", scatter_dimension=0, tiled=True),
        lax.psum_scatter(inner_wgrad, "fsdp", scatter_dimension=0, tiled=True),
        lax.psum_scatter(inner_bgrad, "fsdp", scatter_dimension=0, tiled=True),
        lax.psum_scatter(outer_wgrad, "fsdp", scatter_dimension=0, tiled=True),
        lax.psum_scatter(outer_bgrad, "fsdp", scatter_dimension=0, tiled=True),
        lax.psum_scatter(second_ggrad, "fsdp", scatter_dimension=0, tiled=True),
        lax.psum_scatter(second_sgrad, "fsdp", scatter_dimension=0, tiled=True),
    )
    return (
        output,
        input_grad,
        query_wgrad,
        query_bgrad,
        key_wgrad,
        value_wgrad,
        value_bgrad,
        attn_wgrad,
        attn_bgrad,
        first_ggrad,
        first_sgrad,
        inner_wgrad,
        inner_bgrad,
        outer_wgrad,
        outer_bgrad,
        second_ggrad,
        second_sgrad,
    )


def solution(mesh):
    return jax.shard_map(
        per_device,
        mesh=mesh,
        in_specs=(
            P("fsdp", None),
            P("fsdp"),
            P("fsdp", None),
            P("fsdp", None),
            P("fsdp"),
            P("fsdp", None),
            P("fsdp", None),
            P("fsdp"),
            P("fsdp", None),
            P("fsdp"),
            P("fsdp"),
            P("fsdp"),
            P("fsdp", None),
            P("fsdp"),
            P("fsdp", None),
            P("fsdp"),
            P("fsdp"),
            P("fsdp"),
        ),
        out_specs=(
            P("fsdp", None),
            P("fsdp", None),
            P("fsdp", None),
            P("fsdp"),
            P("fsdp", None),
            P("fsdp", None),
            P("fsdp"),
            P("fsdp", None),
            P("fsdp"),
            P("fsdp"),
            P("fsdp"),
            P("fsdp", None),
            P("fsdp"),
            P("fsdp", None),
            P("fsdp"),
            P("fsdp"),
            P("fsdp"),
        ),
        check_vma=False,
    )
```

profile of v0, /device:TPU:0, one launch (start us, length us, event | category | flops | bytes accessed | tf_op | source)
XLA Modules:
  0.0 1427.9 jit_solution(4981616267195977672)
XLA Ops:
  18.0 42.3 %all-reduce.18 = (bf16[1024]{0:T(1024)(128)(2,1)S(1)}, bf16[1024]{0:T(1024)(128)(2,1)S(1)}, bf16[1024]{0:T(1024)(128)(2,1)S(1)}, bf16[1024]{0:T(1024)(128)(2,1)S...) all-reduce(bf16[1024]{0:T(1024)(128)(2,1)S(1)} %dynamic-update-slic, ...), channel_id=1, replica_groups=mesh['fsdp'=32] {'fsdp'}, use_global_device_ids=true, to_apply=%add.2 | all-reduce | flops 8192 | bytes 32768
  66.1 40.5 %all-gather = bf16[32,1,128]{2,1,0:T(2,128)(2,1)S(1)} all-gather(bf16[1,1,128]{2,1,0:T(2,128)(2,1)S(1)} %bitcast.184), channel_id=1, replica_groups=mesh['fsdp'=32] {'fsdp'}, dimensions={0}, use_global_device_ids=true | all-gather | bytes 8448 | tf_op jit(solution)/shard_map/all_gather | solution.py:123
  142.4 44.2 %all-gather.12.cloned.1.call-done = bf16[1024,1024]{1,0:T(8,128)(2,1)} async-done(((bf16[32,1024]{1,0:T(8,128)(2,1)}), bf16[1024,1024]{1,0:T(8,128)(2,1)}) %all-gather.12.cloned.1.call-update) | async-done | bytes 2097168 | tf_op jit(solution)/shard_map/all_gather | solution.py:115
  199.6 31.5 %while.26 = (s32[]{:T(128)}, bf16[2,512,16,64]{1,3,2,0:T(8,128)(2,1)}, f32[2,16,512]{2,1,0:T(8,128)S(1)}, bf16[2,512,16,64]{1,3,2,0:T(8,128)(2,1)}, s32[2]{0:T(1...) while((s32[]{:T(128)}, ...), condition=%wide.region_3.4_spmd, body=%wide.region_0.3_spmd.sunk | while | flops 1124065792 | bytes 64229508 | solution.py:149
  252.8 70.9 %all-gather.16.cloned.1.call-done = bf16[1024,4096]{1,0:T(8,128)(2,1)} async-done(((bf16[32,4096]{1,0:T(8,128)(2,1)}), bf16[1024,4096]{1,0:T(8,128)(2,1)}) %all-gather.16.cloned.1.call-update) | async-done | bytes 8388624 | tf_op jit(solution)/shard_map/all_gather | solution.py:122
  323.7 48.0 %multiply_convert_fusion.3 = (bf16[1024,4096]{1,0:T(8,128)(2,1)}, f32[1024,4096]{1,0:T(8,128)}, f32[1024,4096]{1,0:T(8,128)}) fusion(f32[4096]{0:T(1024)S(1)} %bitcast.182, bf16[1024,4096]{1,0:T(8,128)(2,1)} %all-gather.16.cloned.1.call-done, bf16[1024,1024]{0,1:T(8,128)(2,1)S(1)} %fusion.66.clone.4), kind=kOutput, calls=%fused_computation.60 | convolution fusion | flops 8866758656 | bytes 52445184 | tf_op jit(solution)/shard_map/dot_general | solution.py:42
  371.7 30.8 %all-gather.18.cloned.1.call-done = bf16[4096,1024]{1,0:T(8,128)(2,1)} async-done(((bf16[128,1024]{1,0:T(8,128)(2,1)}), bf16[4096,1024]{1,0:T(8,128)(2,1)}) %all-gather.18.cloned.1.call-update) | async-done | bytes 8388624 | tf_op jit(solution)/shard_map/all_gather | solution.py:124
  402.5 14.9 %fusion.70 = (f32[1024]{0:T(1024)S(1)}, f32[1024,1024]{0,1:T(8,128)S(1)}) fusion(f32[1024]{0:T(1024)S(1)} %copy-done.49, bf16[1024,4096]{1,0:T(8,128)(2,1)} %get-tuple-element.281, bf16[4096,1024]{1,0:T(8,128)(2,1)} %all-gather.18.cloned.1.call-done, f32[1024]{0:T(1024)S(1)} %copy-done.41, f32[1024]{0:T(1024)S(1)} %copy-done.32, ...), kind=kOutput, calls=%fused_computation.123 | convolution fusion | flops 8597273600 | bytes 25190400 | tf_op jit(solution)/shard_map/dot_general | solution.py:42
  427.9 24.3 %convert_reduce_fusion = (f32[4096]{0:T(1024)}, bf16[1024,4096]{1,0:T(8,128)(2,1)}) fusion(f32[1024,4096]{1,0:T(8,128)} %get-tuple-element.282, f32[1024,4096]{1,0:T(8,128)} %get-tuple-element.290, f32[4096]{0:T(1024)S(1)} %bitcast.183, bf16[1024,1024]{0,1:T(8,128)(2,1)} %get-tuple-element.276, bf16[4096,1024]{1,0:T(8,128)(2,1)} %all-gather.18.cloned.1.call-done), kind=kOutput, calls=%fused_computation.58 | convolution fusion | flops 8661233664 | bytes 52461568 | tf_op jit(solution)/shard_map/dot_general | solution.py:36
  452.3 17.8 %multiply_reduce_fusion.2 = (f32[1024]{0:T(1024)}, f32[1024]{0:T(1024)S(1)}, f32[1024]{0:T(1024)S(1)}, f32[1024]{0:T(1024)}, f32[1024,1024]{0,1:T(8,128)S(1)}) fusion(f32[1024,1024]{0,1:T(8,128)S(1)} %copy-done.5, f32[1024]{0:T(1024)S(1)} %add_rsqrt_fusion.1, f32[1024]{0:T(1024)S(1)} %broadcast_multiply_fusion.5, f32[1024]{0:T(1024)S(1)} %copy-done.32, ...), kind=kOutput, calls=%fused_computation.76 | convolution fusion | flops 8609853440 | bytes 31507456 | tf_op jit(solution)/shard_map/dot_general | solution.py:36
  493.6 97.5 %while.27 = (s32[]{:T(128)}, bf16[2,512,16,64]{1,3,2,0:T(8,128)(2,1)}, bf16[2,512,16,64]{1,3,2,0:T(8,128)(2,1)}, bf16[2,512,16,64]{1,3,2,0:T(8,128)(2,1)}, bf16[...) while((s32[]{:T(128)}, ...), condition=%wide.region_14.15_spmd, body=%wide.region_12.14_spmd.sunk | while | flops 2724717056 | bytes 195205456 | solution.py:222
  504.6 10.6 multiply_reduce_fusion.9
  515.3 12.0 multiply_convert_fusion.5
  543.5 9.6 subtract_exponential_fusion.3
  553.1 10.7 multiply_reduce_fusion.9
  563.8 12.0 multiply_convert_fusion.5
  638.4 16.6 %fusion.63 = f32[1024,4096]{1,0:T(8,128)} fusion(bf16[1024,4096]{1,0:T(8,128)(2,1)} %get-tuple-element.278, f32[1024,1024]{0,1:T(8,128)} %copy-done.4, f32[1024]{0:T(1024)S(1)} %copy-done.42, f32[1024]{0:T(1024)S(1)} %copy-done.33, f32[1024]{0:T(1024)S(1)} %copy-done.35, f32[1024]{0:T(1024)S(1)} %copy-done.31), kind=kOutput, calls=%fused_computation.120 | convolution fusion | flops 8595177472 | bytes 29376512 | tf_op jit(solution)/shard_map/dot_general | solution.py:30
  656.6 14.6 %fusion.71 = f32[4096,1024]{1,0:T(8,128)} fusion(bf16[1024,4096]{1,0:T(8,128)(2,1)} %get-tuple-element.281, bf16[1024,1024]{0,1:T(8,128)(2,1)S(1)} %copy-done.27), kind=kOutput, calls=%fused_computation.124 | convolution fusion | flops 8589934592 | bytes 27262976 | tf_op jit(solution)/shard_map/dot_general | solution.py:30
  675.3 40.9 %all-reduce.17 = (f32[1024]{0:T(1024)S(1)}, f32[1024]{0:T(1024)S(1)}, f32[1024]{0:T(1024)S(1)}, f32[1024]{0:T(1024)S(1)}, f32[1024]{0:T(1024)S(1)}, /*index=5*/f...) all-reduce(f32[1024]{0:T(1024)S(1)} %reduce_sum.184, ...), channel_id=3, replica_groups=mesh['fsdp'=32] {'fsdp'}, use_global_device_ids=true, to_apply=%region_17.18.clone | all-reduce | flops 12288 | bytes 98304
  740.1 32.7 %reduce-scatter.19.cloned.1.call-done = f32[32,1024]{1,0:T(8,128)} async-done(((f32[1024,1024]{1,0:T(8,128)}), f32[32,1024]{1,0:T(8,128)}) %reduce-scatter.19.cloned.1.call-update) | async-done | bytes 131088
  772.8 139.9 %reduce-scatter.21.cloned.1.call-done = f32[32,1024]{1,0:T(8,128)} async-done(((f32[1024,1024]{1,0:T(8,128)}), f32[32,1024]{1,0:T(8,128)}) %reduce-scatter.21.cloned.1.call-update) | async-done | bytes 131088
  912.6 139.4 %reduce-scatter.23.cloned.1.call-done = f32[32,1024]{1,0:T(8,128)} async-done(((f32[1024,1024]{1,0:T(8,128)}), f32[32,1024]{1,0:T(8,128)}) %reduce-scatter.23.cloned.1.call-update) | async-done | bytes 131088
  1052.1 181.7 %reduce-scatter.15.cloned.1.call-done = f32[32,4096]{1,0:T(8,128)} async-done(((f32[1024,4096]{1,0:T(8,128)}), f32[32,4096]{1,0:T(8,128)}) %reduce-scatter.15.cloned.1.call-update) | async-done | bytes 524304 | tf_op jit(solution)/shard_map/reduce_scatter | solution.py:272
  1233.8 187.1 %reduce-scatter.17.cloned.1.call-done = f32[128,1024]{1,0:T(8,128)} async-done(((f32[4096,1024]{1,0:T(8,128)}), f32[128,1024]{1,0:T(8,128)}) %reduce-scatter.17.cloned.1.call-update) | async-done | bytes 524304 | tf_op jit(solution)/shard_map/reduce_scatter | solution.py:274
  (274 shorter events, 270.2 us)
Async XLA Ops:
  7.2 58.9 %copy-start.51 = (bf16[128]{0:T(256)(128)(2,1)S(1)}, bf16[128]{0:T(256)(128)(2,1)}, u32[]{:S(2)}) copy-start(bf16[128]{0:T(256)(128)(2,1)} %param.35) | copy-start | bytes 772
  7.2 101.1 %copy-start.17 = (bf16[1024,1024]{1,0:T(8,128)(2,1)S(1)}, bf16[1024,1024]{1,0:T(8,128)(2,1)}, u32[]{:S(2)}) copy-start(bf16[1024,1024]{1,0:T(8,128)(2,1)} %param.24) | copy-start | bytes 6291460
  7.2 104.9 %all-gather.8.cloned.1.call-start = ((), (), s32[]{:S(2)}) async-start(), calls=%async_computation.6 | async-start | bytes 2162688 | tf_op jit(solution)/shard_map/all_gather | solution.py:116
  7.9 120.5 %all-gather.10.cloned.1.call-start = ((), (), s32[]{:S(2)}) async-start(), calls=%async_computation.7 | async-start | bytes 2162688 | tf_op jit(solution)/shard_map/all_gather | solution.py:113
  8.7 177.9 %all-gather.12.cloned.1.call-start = ((), (), s32[]{:S(2)}) async-start(), calls=%async_computation.8 | async-start | bytes 2162688 | tf_op jit(solution)/shard_map/all_gather | solution.py:115
  9.4 235.2 %all-gather.14.cloned.1.call-start = ((), (), s32[]{:S(2)}) async-start(), calls=%async_computation.9 | async-start | bytes 2162688 | tf_op jit(solution)/shard_map/all_gather | solution.py:118
  10.0 313.7 %all-gather.16.cloned.1.call-start = ((), (), s32[]{:S(2)}) async-start(), calls=%async_computation.10 | async-start | bytes 8650752 | tf_op jit(solution)/shard_map/all_gather | solution.py:122
  10.6 391.9 %all-gather.18.cloned.1.call-start = ((), (), s32[]{:S(2)}) async-start(), calls=%async_computation.11 | async-start | bytes 8650752 | tf_op jit(solution)/shard_map/all_gather | solution.py:124
  11.2 728.9 %reduce-scatter.13.cloned.1.call-start = ((), (), s32[]{:S(2)}) async-start(), calls=%async_computation.12 | async-start | bytes 4325376 | tf_op jit(solution)/shard_map/reduce_scatter | solution.py:268
  60.9 50.0 %copy-start.52 = (s32[2]{0:T(128)S(1)}, s32[2]{0:T(128)}, u32[]{:S(2)}) copy-start(s32[2]{0:T(128)} %param.23) | copy-start | bytes 28
  231.1 13.5 copy-start.50
  250.2 219.9 %copy-start.30 = (f32[1024]{0:T(1024)}, f32[1024]{0:T(1024)S(1)}, u32[]{:S(2)}) copy-start(f32[1024]{0:T(1024)S(1)} %broadcast_multiply_fusion.5) | copy-start | bytes 12292
  250.7 73.0 %copy-start.45 = (f32[32,1,128]{2,1,0:T(1,128)S(1)}, f32[32,1,128]{2,1,0:T(1,128)}, u32[]{:S(2)}) copy-start(f32[32,1,128]{2,1,0:T(1,128)} %convert_element_type.147) | copy-start | bytes 49156
  252.1 218.0 %copy-start.34 = (f32[1024]{0:T(1024)}, f32[1024]{0:T(1024)S(1)}, u32[]{:S(2)}) copy-start(f32[1024]{0:T(1024)S(1)} %add_rsqrt_fusion.1) | copy-start | bytes 12292
  323.7 78.8 %copy-start.49 = (f32[1024]{0:T(1024)S(1)}, f32[1024]{0:T(1024)}, u32[]{:S(2)}) copy-start(f32[1024]{0:T(1024)} %convert_element_type.132) | copy-start | bytes 12292
  427.9 24.3 %copy-start.5 = (f32[1024,1024]{0,1:T(8,128)S(1)}, f32[1024,1024]{0,1:T(8,128)}, u32[]{:S(2)}) copy-start(f32[1024,1024]{0,1:T(8,128)} %copy-done.4) | copy-start | bytes 12582916
  427.9 24.3 %copy-start.10 = (bf16[1024,1024]{0,1:T(8,128)(2,1)S(1)}, bf16[1024,1024]{0,1:T(8,128)(2,1)}, u32[]{:S(2)}) copy-start(bf16[1024,1024]{0,1:T(8,128)(2,1)} %copy.102) | copy-start | bytes 6291460
  493.5 279.3 %reduce-scatter.19.cloned.1.call-start = ((), (), s32[]{:S(2)}) async-start(), calls=%async_computation.15 | async-start | bytes 4325376
  563.8 12.0 copy-start.3
  563.8 12.0 copy-start.19
  606.6 306.0 %reduce-scatter.21.cloned.1.call-start = ((), (), s32[]{:S(2)}) async-start(), calls=%async_computation.16 | async-start | bytes 4325376
  622.0 430.0 %reduce-scatter.23.cloned.1.call-start = ((), (), s32[]{:S(2)}) async-start(), calls=%async_computation.17 | async-start | bytes 4325376
  637.7 596.0 %reduce-scatter.15.cloned.1.call-start = ((), (), s32[]{:S(2)}) async-start(), calls=%async_computation.13 | async-start | bytes 17301504 | tf_op jit(solution)/shard_map/reduce_scatter | solution.py:272
  655.0 765.8 %reduce-scatter.17.cloned.1.call-start = ((), (), s32[]{:S(2)}) async-start(), calls=%async_computation.14 | async-start | bytes 17301504 | tf_op jit(solution)/shard_map/reduce_scatter | solution.py:274
  (52 other events, 210.5 us)
Sparse Core Ops, SparseCore 0:
  10.9 59.4 all-gather.7
  73.2 55.2 all-gather.9
  131.3 55.2 all-gather.11
  189.3 55.3 all-gather.13
  247.4 76.2 all-gather.15
  326.4 76.0 all-gather.17
  493.6 139.3 reduce-scatter.12
  635.9 136.8 reduce-scatter.18
  775.6 136.9 reduce-scatter.20
  915.3 136.6 reduce-scatter.22
  1054.9 178.7 reduce-scatter.14
  1236.5 184.3 reduce-scatter.16
where the time goes:
time: 1430 us
  waiting for transfers between devices  839 us (59%)
  matrix products  278 us (19%)
  blocking collectives  124 us (9%)
  local copies, waits for them, and re-layouts  118 us (8%)
  other arithmetic  51.9 us (4%)
  between operations  15 us (1%)
    unnamed x15, waiting for transfers between devices  316 us
    reduce_scatter x1, waiting for transfers between devices, per_device(): lax.psum_scatter(outer_wgrad, 'fsdp', scatter_dimension=0, tiled=True)  187 us
    reduce_scatter x1, waiting for transfers between devices, per_device(): lax.psum_scatter(inner_wgrad, 'fsdp', scatter_dimension=0, tiled=True)  182 us
    unnamed x2, blocking collectives  83.2 us
    dot_general x5, matrix products, project(): jnp.dot(rows, matrix, preferred_element_type=jnp.float32)  77.8 us
    all_gather x1, waiting for transfers between devices, per_device(): lax.all_gather(inner_weight, 'fsdp', axis=0, tiled=True)  70.9 us
    unnamed x132, local copies, waits for them, and re-layouts  59.2 us
    dot_general x6, matrix products, times_transpose(): lax.dot_general(left, right, (((1,), (1,)), ((), ())), preferred_element_...  58.2 us
  transfers between devices with their start and end apart: 12, of which 10 were waited for; matrix products, arithmetic and copies ran while one was open for 24% of the time, Pallas kernels for 0%

commit v1 on v0

v1 whole, which is shorter than its diff:
```python
from functools import partial

import jax
import jax.numpy as jnp
from jax import lax
from jax.experimental import pallas as pl
from jax.experimental.pallas import tpu as pltpu
from jax.sharding import PartitionSpec as P

HEADS = 16
DHEAD = 64
EPSILON = 1e-05
MASKED = -1e30
SCALE = DHEAD ** (-0.5)
F32 = jnp.float32
BF16 = jnp.bfloat16
BLOCK = 256
VMEM_LIMIT = 60 * 1024 * 1024
SIDES = (0, 2, 4, 6)


def dot(left, right):
    return jnp.dot(left, right, preferred_element_type=F32)


def dot_nt(left, right):
    return lax.dot_general(left, right, (((1,), (1,)), ((), ())), preferred_element_type=F32)


def dot_tn(left, right):
    return lax.dot_general(left, right, (((0,), (0,)), ((), ())), preferred_element_type=F32)


def normalize(rows):
    centred = rows - jnp.mean(rows, axis=-1, keepdims=True)
    factor = lax.rsqrt(jnp.mean(centred * centred, axis=-1, keepdims=True) + EPSILON)
    return centred * factor, factor


def norm_back(grad, normed, factor):
    mean_one = jnp.mean(grad, axis=-1, keepdims=True)
    mean_two = jnp.mean(grad * normed, axis=-1, keepdims=True)
    return factor * (grad - mean_one - normed * mean_two)


def flip(array, bits):
    n = lax.axis_size("fsdp")
    return lax.ppermute(array, "fsdp", [(i, i ^ bits) for i in range(n)])


def after(array, others):
    return lax.optimization_barrier((array,) + tuple(others))[0]


class Weight:
    def __init__(self, pieces, slot, offset, count, rows, columns):
        self.pieces, self.slot, self.offset, self.count = pieces, slot, offset, count
        self.rows, self.columns = rows, columns


def gather_pieces(shard, through):
    n = lax.axis_size("fsdp")
    others = [flip(shard, 8 * k) for k in range(1, n // 8)]
    line = jnp.concatenate([shard] + others) if others else shard
    beside, above = flip(line, 2), flip(line, 4)
    across = flip(above, 2) if through == 2 else flip(beside, 4)
    near = (line, beside, above, across)
    return near + tuple(flip(piece, 1) for piece in near), others


def start_load(weight, refs, target, here, sem, columns=None):
    column = slice(None) if columns is None else columns
    if len(refs) == 1:
        pltpu.make_async_copy(refs[0].at[:, column], target, sem).start()
        return
    count = weight.count
    places = weight.rows // count // 8
    for low, ref in zip(SIDES + tuple(s ^ 1 for s in SIDES), refs):
        for k in range(places):
            owner = here ^ (low ^ (8 * k))
            pltpu.make_async_copy(
                ref.at[pl.ds(k * weight.slot + weight.offset, count), column],
                target.at[pl.ds(pl.multiple_of(owner * count, count), count)],
                sem,
            ).start()


def wait_load(target, sem):
    pltpu.make_async_copy(target, target, sem).wait()


def sum_everywhere(array):
    n = lax.axis_size("fsdp")
    bit = 1
    while bit < n:
        array = array + flip(array, bit)
        bit *= 2
    return array


def add_low(*arrays):
    total = arrays[0].astype(F32)
    for array in arrays[1:]:
        total = total + array.astype(F32)
    return total


def scatter_pieces(keep, send, through):
    low = lambda *arrays: add_low(*arrays).astype(BF16)
    got = flip(send, 1)
    across = low(keep[3], got[3])
    beside, above = None, None
    if through == 2:
        moved = flip(across, 2)
        above = low(keep[2], got[2], moved)
        beside = low(keep[1], got[1])
    else:
        moved = flip(across, 4)
        beside = low(keep[1], got[1], moved)
        above = low(keep[2], got[2])
    from_beside = flip(beside, 2)
    from_above = flip(above, 4)
    places = keep.shape[1]
    pieces = [
        add_low(keep[0, k], got[0, k], from_beside[k], from_above[k]) for k in range(places)
    ]
    arrived = [flip(pieces[k].astype(BF16), 8 * k) for k in range(1, places)]
    return add_low(pieces[0], *arrived)


def operands_of(weights):
    arrays, where = [], []
    for weight in weights:
        places = []
        for piece in weight.pieces:
            for position, array in enumerate(arrays):
                if array is piece:
                    places.append(position)
                    break
            else:
                places.append(len(arrays))
                arrays.append(piece)
        where.append(places)
    return arrays, where


def call(body, grid, info, inputs, specs, weights, outs, out_specs, scratch, flops, name, exps=0):
    arrays, where = operands_of(weights)
    count = len(inputs)

    def kernel(info_ref, *refs):
        ins = refs[:count]
        pieces = refs[count : count + len(arrays)]
        held = [[pieces[p] for p in places] for places in where]
        body(info_ref, ins, held, refs[count + len(arrays) :])

    moved = sum(a.size * a.dtype.itemsize for a in list(inputs) + arrays)
    moved += sum(o.size * o.dtype.itemsize for o in jax.tree.leaves(outs))
    return pl.pallas_call(
        kernel,
        grid_spec=pltpu.PrefetchScalarGridSpec(
            num_scalar_prefetch=1,
            grid=grid,
            in_specs=list(specs) + [pl.BlockSpec(memory_space=pl.ANY)] * len(arrays),
            out_specs=out_specs,
            scratch_shapes=scratch,
        ),
        out_shape=outs,
        compiler_params=pltpu.CompilerParams(
            vmem_limit_bytes=VMEM_LIMIT, dimension_semantics=("arbitrary",) * len(grid)
        ),
        cost_estimate=pl.CostEstimate(flops=flops, bytes_accessed=moved, transcendentals=exps),
        name=name,
    )(info, *inputs, *arrays)


def shape_of(shape, dtype):
    return jax.ShapeDtypeStruct(shape, dtype)


def whole(shape):
    return pl.BlockSpec(shape, lambda *_: (0,) * len(shape))


def by_rows(columns, rows=BLOCK):
    return pl.BlockSpec((rows, columns), lambda i, *_: (i, 0))


def project_qkv(info, tokens, biases, weights):
    rows, width = tokens.shape

    def body(info_ref, ins, held, rest):
        tokens_ref, bias_ref = ins
        out_ref, matrix, sem = rest
        which = pl.program_id(0)

        @pl.when(which == 0)
        def _():
            for i, weight in enumerate(weights):
                start_load(weight, held[i], matrix.at[i], info_ref[0], sem.at[i])

        wait_load(matrix.at[which], sem.at[which])
        factor = jnp.where(which == 0, SCALE, 1.0).astype(F32)
        for start in range(0, rows, BLOCK):
            part = pl.ds(start, BLOCK)
            total = dot(tokens_ref[part, :], matrix[which]) + bias_ref[0]
            out_ref[0, part, :] = (total * factor).astype(BF16)

    return call(
        body,
        (3,),
        info,
        (tokens, biases),
        (whole(tokens.shape), pl.BlockSpec((1, 1, width), lambda i, *_: (i, 0, 0))),
        weights,
        shape_of((3, rows, width), BF16),
        pl.BlockSpec((1, rows, width), lambda i, *_: (i, 0, 0)),
        [pltpu.VMEM((3, width, width), BF16), pltpu.SemaphoreType.DMA((3,))],
        6 * rows * width * width,
        "project_qkv",
    )


def head_masks(span, length):
    lane = lax.broadcasted_iota(jnp.int32, (span, 2 * DHEAD), 1)
    place = lax.broadcasted_iota(jnp.int32, (span, 2 * DHEAD), 0)
    return lane, jnp.where(place < length, 0.0, MASKED).astype(F32)


def marked(array, lane, head, mark):
    own = lane // DHEAD == head
    spare = lane == (1 - head) * DHEAD
    return jnp.where(own, array.astype(F32), jnp.where(spare, mark, 0.0)).astype(BF16)


def attend(info, qkv, seqs):
    _, rows, width = qkv.shape
    span = rows // seqs
    pairs = width // (2 * DHEAD)

    def body(info_ref, ins, held, rest):
        query_ref, key_ref, value_ref = ins
        mixed_ref, logsum_ref = rest
        length = info_ref[1 + pl.program_id(0)]
        lane, mark = head_masks(span, length)
        query, keys = query_ref[0], key_ref[0]
        value_t = value_ref[0].T
        mixed = []
        for head in range(2):
            key_one = marked(keys, lane, head, mark)
            query_one = marked(query, lane, head, 1.0)
            scores = dot_nt(key_one, query_one)
            top = jnp.max(scores, axis=0, keepdims=True)
            expo = jnp.exp(scores - top)
            total = jnp.sum(expo, axis=0, keepdims=True)
            out = dot(value_t[head * DHEAD : (head + 1) * DHEAD], expo.astype(BF16))
            mixed.append(out / total)
            logsum_ref[0, 0, head : head + 1, :] = top + jnp.log(total)
        mixed_ref[...] = jnp.concatenate(mixed, axis=0).T.astype(BF16)

    def block(which):
        return pl.BlockSpec((1, span, 2 * DHEAD), lambda s, p, *_: (which, s, p))

    return call(
        body,
        (seqs, pairs),
        info,
        (qkv, qkv, qkv),
        [block(i) for i in range(3)],
        [],
        (shape_of((rows, width), BF16), shape_of((seqs, pairs, 8, span), F32)),
        (
            pl.BlockSpec((span, 2 * DHEAD), lambda s, p, *_: (s, p)),
            pl.BlockSpec((1, 1, 8, span), lambda s, p, *_: (s, p, 0, 0)),
        ),
        [],
        8 * rows * span * width,
        "attend",
        exps=rows * span * HEADS,
    )


def attend_back(info, qkv, grad_mixed, logsum, seqs):
    _, rows, width = qkv.shape
    span = rows // seqs
    pairs = width // (2 * DHEAD)

    def body(info_ref, ins, held, rest):
        query_ref, key_ref, value_ref, grad_ref, logsum_ref = ins
        step_ref, sums_ref = rest
        length = info_ref[1 + pl.program_id(0)]
        lane, mark = head_masks(span, length)
        query, keys, values, grad = query_ref[0], key_ref[0], value_ref[0], grad_ref[...]
        key_t = keys.T
        query_steps, key_steps, value_steps = [], [], []
        for head in range(2):
            key_one = marked(keys, lane, head, mark)
            query_one = marked(query, lane, head, 1.0)
            value_one = marked(values, lane, head, 0.0)
            scores = dot_nt(key_one, query_one)
            probs = jnp.exp(scores - logsum_ref[0, 0, head : head + 1, :])
            grad_probs = dot_nt(value_one, grad)
            value_steps.append(dot(probs.astype(BF16), grad))
            inner = jnp.sum(grad_probs * probs, axis=0, keepdims=True)
            grad_scores = (probs * (grad_probs - inner)).astype(BF16)
            key_steps.append(dot(grad_scores, query))
            query_steps.append(
                dot(key_t[head * DHEAD : (head + 1) * DHEAD], grad_scores) * SCALE
            )
        first = lane < DHEAD
        query_step = jnp.concatenate(query_steps, axis=0).T.astype(BF16)
        key_step = jnp.where(first, key_steps[0], key_steps[1]).astype(BF16)
        value_step = jnp.where(first, value_steps[0], value_steps[1]).astype(BF16)
        step_ref[0] = query_step
        step_ref[1] = key_step
        step_ref[2] = value_step
        sums_ref[0, 0:1, :] = jnp.sum(query_step.astype(F32), axis=0, keepdims=True)
        sums_ref[0, 1:2, :] = jnp.sum(value_step.astype(F32), axis=0, keepdims=True)

    def block(which):
        return pl.BlockSpec((1, span, 2 * DHEAD), lambda s, p, *_: (which, s, p))

    return call(
        body,
        (seqs, pairs),
        info,
        (qkv, qkv, qkv, grad_mixed, logsum),
        [block(i) for i in range(3)]
        + [
            pl.BlockSpec((span, 2 * DHEAD), lambda s, p, *_: (s, p)),
            pl.BlockSpec((1, 1, 8, span), lambda s, p, *_: (s, p, 0, 0)),
        ],
        [],
        (shape_of((3, rows, width), BF16), shape_of((seqs, 8, width), F32)),
        (
            pl.BlockSpec((3, span, 2 * DHEAD), lambda s, p, *_: (0, s, p)),
            pl.BlockSpec((1, 8, 2 * DHEAD), lambda s, p, *_: (s, 0, p)),
        ),
        [],
        20 * rows * span * width,
        "attend_back",
        exps=rows * span * HEADS,
    )


def project_out(info, mixed, tokens, vectors, weight):
    rows, width = tokens.shape

    def body(info_ref, ins, held, rest):
        mixed_ref, tokens_ref, vector_ref = ins
        normed_ref, low_ref, factor_ref, matrix, sem = rest

        @pl.when(pl.program_id(0) == 0)
        def _():
            start_load(weight, held[0], matrix, info_ref[0], sem)
            wait_load(matrix, sem)

        branch = dot(mixed_ref[...], matrix[...]) + vector_ref[2:3, :]
        normed, factor = normalize(tokens_ref[...].astype(F32) + branch)
        normed_ref[...] = normed
        low_ref[...] = (normed * vector_ref[3:4, :] + vector_ref[4:5, :]).astype(BF16)
        factor_ref[...] = jnp.broadcast_to(factor, factor_ref.shape)

    return call(
        body,
        (rows // BLOCK,),
        info,
        (mixed, tokens, vectors),
        (by_rows(width), by_rows(width), whole(vectors.shape)),
        [weight],
        (shape_of((rows, width), F32), shape_of((rows, width), BF16), shape_of((rows, 128), F32)),
        (by_rows(width), by_rows(width), by_rows(128)),
        [pltpu.VMEM((width, width), BF16), pltpu.SemaphoreType.DMA],
        2 * rows * width * width,
        "project_out",
    )


def gelu_both(hidden):
    size = jnp.abs(hidden) * 0.7071067811865476
    ratio = 1.0 / (1.0 + 0.3275911 * size)
    bell = jnp.exp(-0.5 * (hidden * hidden))
    series = 0.5 * 1.061405429 * ratio + 0.5 * -1.453152027
    series = series * ratio + 0.5 * 1.421413741
    series = series * ratio + 0.5 * -0.284496736
    series = series * ratio + 0.5 * 0.254829592
    tail = series * ratio * bell
    share = jnp.where(hidden >= 0, 1.0 - tail, tail)
    return hidden * share, share + hidden * bell * 0.3989422804014327


def feed_in(info, low, bias, weight):
    rows, width = low.shape
    wide = weight.columns
    part = min(1024, wide)
    steps = wide // part

    def body(info_ref, ins, held, rest):
        low_ref, bias_ref = ins
        active_ref, slope_ref, matrix, sem = rest
        step = pl.program_id(0)

        @pl.when(step == 0)
        def _():
            for i in range(steps):
                start_load(
                    weight, held[0], matrix.at[i], info_ref[0], sem.at[i], pl.ds(i * part, part)
                )

        wait_load(matrix.at[step], sem.at[step])
        for start in range(0, rows, BLOCK):
            some = pl.ds(start, BLOCK)
            hidden = dot(low_ref[some, :], matrix[step]) + bias_ref[...]
            active, slope = gelu_both(hidden)
            active_ref[some, :] = active.astype(BF16)
            slope_ref[some, :] = slope.astype(BF16)

    columns = pl.BlockSpec((rows, part), lambda i, *_: (0, i))
    return call(
        body,
        (steps,),
        info,
        (low, bias),
        (whole(low.shape), pl.BlockSpec((1, part), lambda i, *_: (0, i))),
        [weight],
        (shape_of((rows, wide), BF16), shape_of((rows, wide), BF16)),
        (columns, columns),
        [pltpu.VMEM((steps, width, part), BF16), pltpu.SemaphoreType.DMA((steps,))],
        2 * rows * width * wide,
        "feed_in",
        exps=rows * wide,
    )


def feed_out(info, active, normed, cotangent, vectors, weight, span):
    rows, wide = active.shape
    width = weight.columns

    def body(info_ref, ins, held, rest):
        active_ref, normed_ref, cotangent_ref, vector_ref = ins
        out_ref, second_ref, sums_ref, matrix, sem = rest
        step = pl.program_id(0)

        @pl.when(step == 0)
        def _():
            start_load(weight, held[0], matrix, info_ref[0], sem)
            sums_ref[...] = jnp.zeros_like(sums_ref)
            wait_load(matrix, sem)

        middle = normed_ref[...] * vector_ref[3:4, :] + vector_ref[4:5, :]
        branch = dot(active_ref[...], matrix[...]) + vector_ref[5:6, :]
        second, factor = normalize(middle + branch)
        gain = vector_ref[6:7, :]
        out_ref[...] = (second * gain + vector_ref[7:8, :]).astype(BF16)
        places = step * BLOCK + lax.broadcasted_iota(jnp.int32, (BLOCK, 1), 0)
        sequence = (step * BLOCK) // span
        length = info_ref[1 + sequence]
        valid = places - sequence * span < length
        grad = jnp.where(valid, cotangent_ref[...].astype(F32), 0.0)
        sums_ref[0:1, :] += jnp.sum(grad * second, axis=0, keepdims=True)
        sums_ref[1:2, :] += jnp.sum(grad, axis=0, keepdims=True)
        back = norm_back(grad * gain, second, factor)
        second_ref[...] = back
        sums_ref[2:3, :] += jnp.sum(back.astype(BF16).astype(F32), axis=0, keepdims=True)

    return call(
        body,
        (rows // BLOCK,),
        info,
        (active, normed, cotangent, vectors),
        (by_rows(wide), by_rows(width), by_rows(width), whole(vectors.shape)),
        [weight],
        (
            shape_of((rows, width), BF16),
            shape_of((rows, width), F32),
            shape_of((8, width), F32),
        ),
        (by_rows(width), by_rows(width), whole((8, width))),
        [pltpu.VMEM((wide, width), BF16), pltpu.SemaphoreType.DMA],
        2 * rows * width * wide,
        "feed_out",
    )


def feed_back(info, second, slope, normed, factor, vectors, outer, inner, attn):
    rows, width = second.shape
    wide = slope.shape[1]
    part = min(1024, wide)

    def body(info_ref, ins, held, rest):
        second_ref, slope_ref, normed_ref, factor_ref, vector_ref = ins
        hidden_ref, proj_ref, mixed_ref, bias_ref, sums_ref, big, wide_m, small, sem = rest
        step = pl.program_id(0)

        @pl.when(step == 0)
        def _():
            start_load(outer, held[0], big, info_ref[0], sem.at[0])
            start_load(inner, held[1], wide_m, info_ref[0], sem.at[1])
            start_load(attn, held[2], small, info_ref[0], sem.at[2])
            sums_ref[...] = jnp.zeros_like(sums_ref)
            bias_ref[...] = jnp.zeros_like(bias_ref)
            wait_load(big, sem.at[0])

        branch = second_ref[...].astype(BF16)
        for start in range(0, wide, part):
            some = pl.ds(start, part)
            grad = dot_nt(branch, big[some, :]) * slope_ref[:, some].astype(F32)
            grad = grad.astype(BF16)
            hidden_ref[:, some] = grad
            bias_ref[0:1, some] += jnp.sum(grad.astype(F32), axis=0, keepdims=True)

        @pl.when(step == 0)
        def _():
            wait_load(wide_m, sem.at[1])
            wait_load(small, sem.at[2])

        middle = second_ref[...] + dot_nt(hidden_ref[...], wide_m[...])
        normed = normed_ref[...]
        sums_ref[0:1, :] += jnp.sum(middle * normed, axis=0, keepdims=True)
        sums_ref[1:2, :] += jnp.sum(middle, axis=0, keepdims=True)
        first = norm_back(middle * vector_ref[3:4, :], normed, factor_ref[:, 0:1])
        proj = first.astype(BF16)
        proj_ref[...] = proj
        sums_ref[2:3, :] += jnp.sum(proj.astype(F32), axis=0, keepdims=True)
        mixed_ref[...] = dot_nt(proj, small[...]).astype(BF16)

    return call(
        body,
        (rows // BLOCK,),
        info,
        (second, slope, normed, factor, vectors),
        (by_rows(width), by_rows(wide), by_rows(width), by_rows(128), whole(vectors.shape)),
        [outer, inner, attn],
        (
            shape_of((rows, wide), BF16),
            shape_of((rows, width), BF16),
            shape_of((rows, width), BF16),
            shape_of((8, wide), F32),
            shape_of((8, width), F32),
        ),
        (by_rows(wide), by_rows(width), by_rows(width), whole((8, wide)), whole((8, width))),
        [
            pltpu.VMEM((wide, width), BF16),
            pltpu.VMEM((width, wide), BF16),
            pltpu.VMEM((width, width), BF16),
            pltpu.SemaphoreType.DMA((3,)),
        ],
        4 * rows * width * wide + 2 * rows * width * width,
        "feed_back",
    )


def input_back(info, proj, steps, weights):
    rows, width = proj.shape

    def body(info_ref, ins, held, rest):
        proj_ref, step_ref = ins
        out_ref, matrix, sem = rest

        @pl.when(pl.program_id(0) == 0)
        def _():
            for i, weight in enumerate(weights):
                start_load(weight, held[i], matrix.at[i], info_ref[0], sem.at[i])
            for i in range(3):
                wait_load(matrix.at[i], sem.at[i])

        total = proj_ref[...].astype(F32)
        for i in range(3):
            total += dot_nt(step_ref[i], matrix[i])
        out_ref[...] = total.astype(BF16)

    return call(
        body,
        (rows // BLOCK,),
        info,
        (proj, steps),
        (by_rows(width), pl.BlockSpec((3, BLOCK, width), lambda i, *_: (0, i, 0))),
        weights,
        shape_of((rows, width), BF16),
        by_rows(width),
        [pltpu.VMEM((3, width, width), BF16), pltpu.SemaphoreType.DMA((3,))],
        6 * rows * width * width,
        "input_back",
    )


def weight_grad(info, left, right, places, name):
    rows, height = left.shape
    if right.ndim == 2:
        right = right[None]
    parts, _, width = right.shape
    tall = height // places
    slot = tall // 8
    part = min(1024, width)
    chunk = max(slot, 256)

    def body(info_ref, ins, held, rest):
        left_ref, right_ref = ins
        keep_ref, send_ref, held_ref = rest
        here = info_ref[0]
        for start in range(0, tall, chunk):
            total = dot_tn(left_ref[:, start : start + chunk], right_ref[0].astype(BF16))
            for k in range(chunk // slot):
                held_ref[start // slot + k] = total[k * slot : (k + 1) * slot].astype(BF16)
        core = here & 1
        for side in range(4):
            place = ((here >> 1) & 3) ^ side
            keep_ref[side, 0] = held_ref[2 * place + core]
            send_ref[side, 0] = held_ref[2 * place + 1 - core]

    out = shape_of((4, places, parts * slot, width), BF16)
    block = pl.BlockSpec((4, 1, slot, part), lambda z, w, c, *_: (0, z, w, c))
    return call(
        body,
        (places, parts, width // part),
        info,
        (left, right),
        (
            pl.BlockSpec((rows, tall), lambda z, w, c, info: (0, z ^ (info[0] >> 3))),
            pl.BlockSpec((1, rows, part), lambda z, w, c, *_: (w, 0, c)),
        ),
        [],
        (out, out),
        (block, block),
        [pltpu.VMEM((8, slot, part), BF16)],
        2 * rows * height * parts * width,
        name,
    )


def per_device(
    tokens,
    lengths,
    cotangent,
    query_weight,
    query_bias,
    key_weight,
    value_weight,
    value_bias,
    attn_weight,
    attn_bias,
    first_gain,
    first_shift,
    inner_weight,
    inner_bias,
    outer_weight,
    outer_bias,
    second_gain,
    second_shift,
):
    n = lax.axis_size("fsdp")
    here = lax.axis_index("fsdp").astype(jnp.int32)
    seqs = lengths.shape[0]
    rows, width = tokens.shape
    wide = inner_weight.shape[1]
    span = rows // seqs
    own = query_weight.shape[0]
    tall = outer_weight.shape[0]
    staged = n in (8, 16, 32) and own % 16 == 0
    info = jnp.concatenate([here[None], lengths])

    small = (
        query_bias,
        value_bias,
        attn_bias,
        first_gain,
        first_shift,
        outer_bias,
        second_gain,
        second_shift,
        inner_bias,
    )
    small = jnp.concatenate(small)[None]
    table = lax.dynamic_update_slice(jnp.zeros((n, small.shape[1]), BF16), small, (here, 0))
    table = sum_everywhere(table).astype(F32)
    vectors = table[:, : 8 * own].reshape(n, 8, own).transpose(1, 0, 2).reshape(8, width)
    wide_bias = table[:, 8 * own :].reshape(1, wide)

    if staged:
        one = jnp.concatenate([query_weight, key_weight, value_weight])
        pieces, got = gather_pieces(one, 2)
        qkv_weights = [Weight(pieces, 3 * own, i * own, own, width, width) for i in range(3)]
        pieces, got = gather_pieces(after(attn_weight, got), 4)
        attn = Weight(pieces, own, 0, own, width, width)
        pieces, got = gather_pieces(after(inner_weight, got), 4)
        inner = Weight(pieces, own, 0, own, width, wide)
        pieces, got = gather_pieces(after(outer_weight, got), 2)
        outer = Weight(pieces, tall, 0, tall, wide, width)
    else:
        full = lambda w: lax.all_gather(w, "fsdp", axis=0, tiled=True)
        view = lambda w: Weight((full(w),), 0, 0, w.shape[0], n * w.shape[0], w.shape[1])
        qkv_weights = [view(w) for w in (query_weight, key_weight, value_weight)]
        attn, inner, outer = view(attn_weight), view(inner_weight), view(outer_weight)

    biases = jnp.stack([vectors[0:1], jnp.zeros((1, width), F32), vectors[1:2]])
    qkv = project_qkv(info, tokens, biases, qkv_weights)
    mixed, logsum = attend(info, qkv, seqs)
    normed, low, factor = project_out(info, mixed, tokens, vectors, attn)
    active, slope = feed_in(info, low, wide_bias, inner)
    output, second, sums_second = feed_out(info, active, normed, cotangent, vectors, outer, span)

    def reduced(left, right, name, through):
        if staged:
            keep, send = weight_grad(info, left, right, n // 8, name)
            return scatter_pieces(keep, send, through)
        right = right if right.ndim == 3 else right[None]
        sums = [dot_tn(left, r.astype(BF16)) for r in right]
        out = [lax.psum_scatter(s, "fsdp", scatter_dimension=0, tiled=True) for s in sums]
        return jnp.concatenate(out)

    outer_wgrad = reduced(active, second.astype(BF16), "grad_outer", 2)
    grad_hidden, grad_proj, grad_mixed, sums_wide, sums_first = feed_back(
        info, second, slope, normed, factor, vectors, outer, inner, attn
    )
    inner_wgrad = reduced(low, grad_hidden, "grad_inner", 4)
    attn_wgrad = reduced(mixed, grad_proj, "grad_attn", 4)
    steps, sums_attn = attend_back(info, qkv, grad_mixed, logsum, seqs)
    qkv_wgrad = reduced(tokens, steps, "grad_qkv", 2)
    input_grad = input_back(info, grad_proj, steps, qkv_weights)

    early = jnp.concatenate([sums_second[:3], sums_first[:3], sums_wide[:1].reshape(-1, width)])
    early = sum_everywhere(early)
    late = sum_everywhere(jnp.sum(sums_attn, axis=0)[:2])
    mine = lax.dynamic_slice(early[:6], (0, here * own), (6, own))
    inner_bgrad = lax.dynamic_slice(early[6:].reshape(-1), (here * tall,), (tall,))
    last = lax.dynamic_slice(late, (0, here * own), (2, own))
    return (
        output,
        input_grad,
        qkv_wgrad[:own],
        last[0],
        qkv_wgrad[own : 2 * own],
        qkv_wgrad[2 * own :],
        last[1],
        attn_wgrad,
        mine[5],
        mine[3],
        mine[4],
        inner_wgrad,
        inner_bgrad,
        outer_wgrad,
        mine[2],
        mine[0],
        mine[1],
    )


def solution(mesh):
    rows, vector = P("fsdp", None), P("fsdp")
    return jax.shard_map(
        per_device,
        mesh=mesh,
        in_specs=(
            rows,
            vector,
            rows,
            rows,
            vector,
            rows,
            rows,
            vector,
            rows,
            vector,
            vector,
            vector,
            rows,
            vector,
            rows,
            vector,
            vector,
            vector,
        ),
        out_specs=(
            rows,
            rows,
            rows,
            vector,
            rows,
            rows,
            vector,
            rows,
            vector,
            vector,
            vector,
            rows,
            vector,
            rows,
            vector,
            vector,
            vector,
        ),
        check_vma=False,
    )
```

time: 1430 us -> 592 us (0.41)
  waiting for transfers between devices: 839 us -> 198 us
  matrix products: 278 us -> 0 us
  Pallas kernels: 0 us -> 239 us
  blocking collectives: 124 us -> 0 us
  local copies, waits for them, and re-layouts: 118 us -> 19.5 us
  starting transfers between devices: 1.19 us -> 94.7 us
  other arithmetic: 51.9 us -> 32.4 us
    reduce_scatter x3 -> x0, waiting for transfers between devices: 369 us -> none  [the longest x1 187 us: per_device(): lax.psum_scatter(outer_wgrad, 'fsdp', scatter_dimension=0, tiled=True)]
    unnamed x15 -> x0, waiting for transfers between devices: 316 us -> none
    dot_general x32 -> x0, matrix products: 278 us -> none  [the longest x5 77.8 us: project(): jnp.dot(rows, matrix, preferred_element_type=jnp.float32)]
    pallas_call x0 -> x12, Pallas kernels: none -> 239 us  [call(): pl.pallas_call(kernel, grid_spec=pltpu.PrefetchScalarGridSpec(num_scalar_...]
    ppermute x0 -> x83, waiting for transfers between devices: none -> 198 us  [flip(): return lax.ppermute(array, 'fsdp', [(i, i ^ bits) for i in range(n)])]
    all_gather x6 -> x0, waiting for transfers between devices: 155 us -> none  [the longest x1 70.9 us: per_device(): lax.all_gather(inner_weight, 'fsdp', axis=0, tiled=True)]
    ppermute x0 -> x83, starting transfers between devices: none -> 94.7 us  [flip(): return lax.ppermute(array, 'fsdp', [(i, i ^ bits) for i in range(n)])]
    unnamed x2 -> x0, blocking collectives: 83.2 us -> none
  transfers between devices with their start and end apart: 12 -> 83, of which waited for: 10 -> 31; matrix products, arithmetic and copies ran while one was open for 24% -> 7% of each run, Pallas kernels for 0% -> 35%
where the time goes in v1:
time: 592 us; the launch traced here: 585 us
  Pallas kernels  239 us (40%)
  waiting for transfers between devices  198 us (33%)
  starting transfers between devices  94.7 us (16%)
  other arithmetic  32.4 us (5%)
  local copies, waits for them, and re-layouts  19.5 us (3%)
    pallas_call x12, Pallas kernels, call(): pl.pallas_call(kernel, grid_spec=pltpu.PrefetchScalarGridSpec(num_scalar_...  239 us
    ppermute x83, waiting for transfers between devices, flip(): return lax.ppermute(array, 'fsdp', [(i, i ^ bits) for i in range(n)])  198 us
    ppermute x83, starting transfers between devices, flip(): return lax.ppermute(array, 'fsdp', [(i, i ^ bits) for i in range(n)])  94.7 us
    convert_element_type x8, other arithmetic, scatter_pieces(): low = lambda *arrays: add_low(*arrays).astype(BF16)  14.4 us
  transfers between devices with their start and end apart: 83, of which 31 were waited for; matrix products, arithmetic and copies ran while one was open for 7% of the time, Pallas kernels for 35%

profile of v1, /device:TPU:0, one launch (start us, length us, event | category | flops | bytes accessed | tf_op | source)
XLA Modules:
  0.0 585.4 jit_solution(5674332630275972458)
XLA Ops:
  55.5 9.5 %collective-permute-done.26 = bf16[32,4096]{1,0:T(8,128)(2,1)S(1)} collective-permute-done((bf16[32,4096]{1,0:T(8,128)(2,1)S(1)}, bf16[32,4096]{1,0:T(8,128)(2,1)S(1)}, u32[]{:S(2)}, u32[]{:S(2)}) %collective-permute-start.26) | collective-permute-done | bytes 262176 | tf_op jit(solution)/shard_map/ppermute | solution.py:48
  79.1 13.5 %collective-permute-done.36 = bf16[128,1024]{1,0:T(8,128)(2,1)S(1)} collective-permute-done((bf16[128,1024]{1,0:T(8,128)(2,1)S(1)}, bf16[128,1024]{1,0:T(8,128)(2,1)S(1)}, u32[]{:S(2)}, u32[]{:S(2)}) %collective-permute-start.36) | collective-permute-done | bytes 262176 | tf_op jit(solution)/shard_map/ppermute | solution.py:48
  102.2 18.8 %collective-permute-done.28.refs_3_.refs_14_ = bf16[128,4096]{1,0:T(8,128)(2,1)S(1)} collective-permute-done((bf16[128,4096]{1,0:T(8,128)(2,1)S(1)}, bf16[128,4096]{1,0:T(8,128)(2,1)S(1)}, u32[]{:S(2)}, u32[]{:S(2)}) %collective-permute-start.28) | collective-permute-done | bytes 1048608 | tf_op jit(solution)/shard_map/ppermute | solution.py:48
  122.1 15.1 %collective-permute-done.10.refs_5_ = bf16[384,1024]{1,0:T(8,128)(2,1)S(1)} collective-permute-done((bf16[384,1024]{1,0:T(8,128)(2,1)S(1)}, bf16[384,1024]{1,0:T(8,128)(2,1)S(1)}, u32[]{:S(2)}, u32[]{:S(2)}) %collective-permute-start.10) | collective-permute-done | bytes 786464 | tf_op jit(solution)/shard_map/ppermute | solution.py:48
  148.2 18.0 %collective-permute-done.30.refs_5_.refs_16_ = bf16[128,4096]{1,0:T(8,128)(2,1)} collective-permute-done((bf16[128,4096]{1,0:T(8,128)(2,1)S(1)}, bf16[128,4096]{1,0:T(8,128)(2,1)}, u32[]{:S(2)}, u32[]{:S(2)}) %collective-permute-start.30) | collective-permute-done | bytes 1048608 | tf_op jit(solution)/shard_map/ppermute | solution.py:48
  166.2 12.9 %project_qkv.1.refs_0_.refs_1_.refs_2_ = bf16[3,1024,1024]{2,1,0:T(8,128)(2,1)} custom-call(s32[3]{0:T(128)} %pad_add_fusion.info_ref, bf16[1024,1024]{1,0:T(8,128)(2,1)} %refs_0_.3, f32[3,1,1024]{2,1,0:T(1,128)} %pad_maximum_fusion.1.refs_1_, bf16[384,1024]{1,0:T(8,128)(2,1)} %constant_dynamic-update-slice_fusion.3.refs_2_, bf16[384,1024]{1,0:T(8,128)(2,1)} %copy-done.18, ...), custom_call_target="tpu_custom_call" | custom-call | flops 6442450944 | bytes 14692352 | tf_op jit(solution)/shard_map/project_qkv/pallas_call | solution.py:159
  180.2 6.6 %collective-permute-done.40.refs_7_.refs_8_ = bf16[512,1024]{1,0:T(8,128)(2,1)} collective-permute-done((bf16[512,1024]{1,0:T(8,128)(2,1)}, bf16[512,1024]{1,0:T(8,128)(2,1)}, u32[]{:S(2)}, u32[]{:S(2)}) %collective-permute-start.40) | collective-permute-done | bytes 1048608 | tf_op jit(solution)/shard_map/ppermute | solution.py:48
  186.8 23.2 %attend.1 = (bf16[1024,1024]{1,0:T(8,128)(2,1)}, f32[2,8,8,512]{3,2,1,0:T(8,128)}) custom-call(s32[3]{0:T(128)} %pad_add_fusion.info_ref, bf16[3,1024,1024]{2,1,0:T(8,128)(2,1)} %project_qkv.1.refs_0_.refs_1_.refs_2_, bf16[3,1024,1024]{2,1,0:T(8,128)(2,1)} %project_qkv.1.refs_0_.refs_1_.refs_2_, bf16[3,1024,1024]{2,1,0:T(8,128)(2,1)} %project_qkv.1.refs_0_.refs_1_.refs_2_), custom_call_target="tpu_custom_call" | custom-call | flops 4294967296 | bytes 21233664 | tf_op jit(solution)/shard_map/attend/pallas_call | solution.py:159
  210.0 9.6 %project_out.1 = (f32[1024,1024]{1,0:T(8,128)}, bf16[1024,1024]{1,0:T(8,128)(2,1)}, f32[1024,128]{1,0:T(8,128)}) custom-call(s32[3]{0:T(128)} %pad_add_fusion.info_ref, bf16[1024,1024]{1,0:T(8,128)(2,1)} %get-tuple-element.45.refs_0_, bf16[1024,1024]{1,0:T(8,128)(2,1)} %refs_0_.3, f32[8,1024]{1,0:T(8,128)} %reshape.210.refs_2_.refs_3_.refs_4_, ...), custom_call_target="tpu_custom_call" | custom-call | flops 2147483648 | bytes 13139968 | tf_op jit(solution)/shard_map/project_out/pallas_call | solution.py:159
  219.6 29.3 %feed_in.1 = (bf16[1024,4096]{1,0:T(8,128)(2,1)}, bf16[1024,4096]{1,0:T(8,128)(2,1)}) custom-call(s32[3]{0:T(128)} %pad_add_fusion.info_ref, bf16[1024,1024]{1,0:T(8,128)(2,1)} %get-tuple-element.47.refs_0_, f32[1,4096]{1,0:T(1,128)} %bitcast.255, bf16[128,4096]{1,0:T(8,128)(2,1)} %copy-done.7, bf16[128,4096]{1,0:T(8,128)(2,1)} %copy-done.13, ...), custom_call_target="tpu_custom_call" | custom-call | flops 8589934592 | bytes 27279360 | tf_op jit(solution)/shard_map/feed_in/pallas_call | solution.py:159
  250.2 20.7 %feed_out.1 = (bf16[1024,1024]{1,0:T(8,128)(2,1)}, f32[1024,1024]{1,0:T(8,128)}, f32[8,1024]{1,0:T(8,128)}) custom-call(s32[3]{0:T(128)} %pad_add_fusion.info_ref, bf16[1024,4096]{1,0:T(8,128)(2,1)} %get-tuple-element.49.refs_0_, f32[1024,1024]{1,0:T(8,128)} %get-tuple-element.50.refs_1_.refs_2_, bf16[1024,1024]{1,0:T(8,128)(2,1)} %refs_2_.1, ...), custom_call_target="tpu_custom_call" | custom-call | flops 8589934592 | bytes 29425664 | tf_op jit(solution)/shard_map/feed_out/pallas_call | solution.py:159
  274.8 14.5 %grad_outer.1 = (bf16[4,4,128,1024]{3,2,1,0:T(8,128)(2,1)}, bf16[4,4,128,1024]{3,2,1,0:T(8,128)(2,1)}) custom-call(s32[3]{0:T(128)} %pad_add_fusion.info_ref, bf16[1024,4096]{1,0:T(8,128)(2,1)} %get-tuple-element.49.refs_0_, bf16[1,1024,1024]{2,1,0:T(8,128)(2,1)} %convert_bitcast_fusion.refs_1_), custom_call_target="tpu_custom_call" | custom-call | flops 8589934592 | bytes 18874368 | tf_op jit(solution)/shard_map/grad_outer/pallas_call | solution.py:159
  289.8 32.2 %feed_back.1 = (bf16[1024,4096]{1,0:T(8,128)(2,1)}, bf16[1024,1024]{1,0:T(8,128)(2,1)}, bf16[1024,1024]{1,0:T(8,128)(2,1)}, f32[8,4096]{1,0:T(8,128)}, f32[8,1024]{1,0:T(8,128)}) custom-call(s32[3]{0:T(128)} %pad_add_fusion.info_ref, f32[1024,1024]{1,0:T(8,128)} %get-tuple-element.53.refs_0_, bf16[1024,4096]{1,0:T(8,128)(2,1)} %get-tuple-element.54.refs_1_, ...), custom_call_target="tpu_custom_call" | custom-call | flops 19327352832 | bytes 48955392 | tf_op jit(solution)/shard_map/feed_back/pallas_call | solution.py:159
  322.0 32.9 %attend_back.1 = (bf16[3,1024,1024]{2,1,0:T(8,128)(2,1)}, f32[2,8,1024]{2,1,0:T(8,128)}) custom-call(s32[3]{0:T(128)} %pad_add_fusion.info_ref, bf16[3,1024,1024]{2,1,0:T(8,128)(2,1)} %project_qkv.1.refs_0_.refs_1_.refs_2_, bf16[3,1024,1024]{2,1,0:T(8,128)(2,1)} %project_qkv.1.refs_0_.refs_1_.refs_2_, ...), custom_call_target="tpu_custom_call" | custom-call | flops 10737418240 | bytes 27590656 | tf_op jit(solution)/shard_map/attend_back/pallas_call | solution.py:159
  354.9 18.8 %grad_qkv.1 = (bf16[4,4,96,1024]{3,2,1,0:T(8,128)(2,1)}, bf16[4,4,96,1024]{3,2,1,0:T(8,128)(2,1)}) custom-call(s32[3]{0:T(128)} %pad_add_fusion.info_ref, bf16[1024,1024]{1,0:T(8,128)(2,1)} %refs_0_.3, bf16[3,1024,1024]{2,1,0:T(8,128)(2,1)} %get-tuple-element.59.refs_1_), custom_call_target="tpu_custom_call" | custom-call | flops 6442450944 | bytes 14680064 | tf_op jit(solution)/shard_map/grad_qkv/pallas_call | solution.py:159
  374.0 24.2 %grad_inner.1 = (bf16[4,4,32,4096]{3,2,1,0:T(8,128)(2,1)}, bf16[4,4,32,4096]{3,2,1,0:T(8,128)(2,1)}) custom-call(s32[3]{0:T(128)} %pad_add_fusion.info_ref, bf16[1024,1024]{1,0:T(8,128)(2,1)} %get-tuple-element.47.refs_0_, bf16[1,1024,4096]{2,1,0:T(8,128)(2,1)} %bitcast.257), custom_call_target="tpu_custom_call" | custom-call | flops 8589934592 | bytes 18874368 | tf_op jit(solution)/shard_map/grad_inner/pallas_call | solution.py:159
  417.6 6.9 %grad_attn.1 = (bf16[4,4,32,1024]{3,2,1,0:T(8,128)(2,1)}, bf16[4,4,32,1024]{3,2,1,0:T(8,128)(2,1)}) custom-call(s32[3]{0:T(128)} %pad_add_fusion.info_ref, bf16[1024,1024]{1,0:T(8,128)(2,1)} %get-tuple-element.45.refs_0_, bf16[1,1024,1024]{2,1,0:T(8,128)(2,1)} %bitcast.258), custom_call_target="tpu_custom_call" | custom-call | flops 2147483648 | bytes 6291456 | tf_op jit(solution)/shard_map/grad_attn/pallas_call | solution.py:159
  426.4 13.5 %input_back.1 = bf16[1024,1024]{1,0:T(8,128)(2,1)} custom-call(s32[3]{0:T(128)} %pad_add_fusion.info_ref, bf16[1024,1024]{1,0:T(8,128)(2,1)} %get-tuple-element.56.refs_0_, bf16[3,1024,1024]{2,1,0:T(8,128)(2,1)} %get-tuple-element.59.refs_1_, bf16[384,1024]{1,0:T(8,128)(2,1)} %constant_dynamic-update-slice_fusion.3.refs_2_, bf16[384,1024]{1,0:T(8,128)(2,1)} %copy-done.18, ...), custom_call_target="tpu_custom_call" | custom-call | flops 6442450944 | bytes 16777216 | tf_op jit(solution)/shard_map/input_back/pallas_call | solution.py:159
  452.9 6.6 %collective-permute-done.58 = bf16[4,32,1024]{2,1,0:T(8,128)(2,1)S(1)} collective-permute-done((bf16[4,32,1024]{2,1,0:T(8,128)(2,1)S(1)}, bf16[4,32,1024]{2,1,0:T(8,128)(2,1)S(1)}, u32[]{:S(2)}, u32[]{:S(2)}) %collective-permute-start.58) | collective-permute-done | bytes 262176 | tf_op jit(solution)/shard_map/ppermute | solution.py:48
  461.4 6.8 %collective-permute-done.47 = bf16[4,96,1024]{2,1,0:T(8,128)(2,1)S(1)} collective-permute-done((bf16[4,96,1024]{2,1,0:T(8,128)(2,1)S(1)}, bf16[4,96,1024]{2,1,0:T(8,128)(2,1)S(1)}, u32[]{:S(2)}, u32[]{:S(2)}) %collective-permute-start.47) | collective-permute-done | bytes 786464 | tf_op jit(solution)/shard_map/ppermute | solution.py:48
  481.3 9.3 %collective-permute-done.46 = bf16[4,96,1024]{2,1,0:T(8,128)(2,1)S(1)} collective-permute-done((bf16[4,96,1024]{2,1,0:T(8,128)(2,1)S(1)}, bf16[4,96,1024]{2,1,0:T(8,128)(2,1)S(1)}, u32[]{:S(2)}, u32[]{:S(2)}) %collective-permute-start.46) | collective-permute-done | bytes 786464 | tf_op jit(solution)/shard_map/ppermute | solution.py:48
  496.3 14.6 %collective-permute-done.78 = bf16[4,128,1024]{2,1,0:T(8,128)(2,1)S(1)} collective-permute-done((bf16[4,128,1024]{2,1,0:T(8,128)(2,1)S(1)}, bf16[4,128,1024]{2,1,0:T(8,128)(2,1)S(1)}, u32[]{:S(2)}, u32[]{:S(2)}) %collective-permute-start.78) | collective-permute-done | bytes 1048608 | tf_op jit(solution)/shard_map/ppermute | solution.py:48
  548.2 13.2 %collective-permute-done.72 = bf16[4,32,4096]{2,1,0:T(8,128)(2,1)S(1)} collective-permute-done((bf16[4,32,4096]{2,1,0:T(8,128)(2,1)S(1)}, bf16[4,32,4096]{2,1,0:T(8,128)(2,1)S(1)}, u32[]{:S(2)}, u32[]{:S(2)}) %collective-permute-start.72) | collective-permute-done | bytes 1048608 | tf_op jit(solution)/shard_map/ppermute | solution.py:48
  574.6 8.6 %collective-permute-done.74 = bf16[32,4096]{1,0:T(8,128)(2,1)S(1)} collective-permute-done((bf16[32,4096]{1,0:T(8,128)(2,1)S(1)}, bf16[32,4096]{1,0:T(8,128)(2,1)S(1)}, u32[]{:S(2)}, u32[]{:S(2)}) %collective-permute-start.74) | collective-permute-done | bytes 262176 | tf_op jit(solution)/shard_map/ppermute | solution.py:48
  (297 shorter events, 204.5 us)
Async XLA Ops:
  31.2 37.5 %collective-permute-start.4 = (bf16[32,384]{1,0:T(8,128)(2,1)S(1)}, bf16[32,384]{1,0:T(8,128)(2,1)S(1)}, u32[]{:S(2)}, u32[]{:S(2)}) collective-permute-start(bf16[32,384]{1,0:T(8,128)(2,1)S(1)} %add.356), channel_id=1, source_target_pairs={{0,16},{1,17},{2,18},{3,19},{4,20},{5,21},{6,22},{7,23},{8,24},{9,... | collective-permute-start | bytes 73736 | tf_op jit(solution)/shard_map/ppermute | solution.py:48
  68.7 27.8 %collective-permute-start.9 = (bf16[384,1024]{1,0:T(8,128)(2,1)}, bf16[384,1024]{1,0:T(8,128)(2,1)S(1)}, u32[]{:S(2)}, u32[]{:S(2)}) collective-permute-start(bf16[384,1024]{1,0:T(8,128)(2,1)} %constant_dynamic-update-slice_fusion.3.refs_2_), channel_id=1, source_target_pairs={{0,4},{1,5},{2,6},{3,7},{4,0},{5,1},{6,2},{7,3},{8,12},{9,13},{10,... | collective-permute-start | bytes 2359304 | tf_op jit(solution)/shard_map/ppermute | solution.py:48
  70.3 27.7 %collective-permute-start.8 = (bf16[384,1024]{1,0:T(8,128)(2,1)}, bf16[384,1024]{1,0:T(8,128)(2,1)S(1)}, u32[]{:S(2)}, u32[]{:S(2)}) collective-permute-start(bf16[384,1024]{1,0:T(8,128)(2,1)} %constant_dynamic-update-slice_fusion.3.refs_2_), channel_id=1, source_target_pairs={{0,2},{1,3},{2,0},{3,1},{4,6},{5,7},{6,4},{7,5},{8,10},{9,11},{10,... | collective-permute-start | bytes 2359304 | tf_op jit(solution)/shard_map/ppermute | solution.py:48
  96.5 40.8 %collective-permute-start.10 = (bf16[384,1024]{1,0:T(8,128)(2,1)S(1)}, bf16[384,1024]{1,0:T(8,128)(2,1)S(1)}, u32[]{:S(2)}, u32[]{:S(2)}) collective-permute-start(bf16[384,1024]{1,0:T(8,128)(2,1)S(1)} %collective-permute-done.9.refs_4_), channel_id=1, source_target_pairs={{0,2},{1,3},{2,0},{3,1},{4,6},{5,7},{6,4},{7,5},{8,10},{9,11},{10,... | collective-permute-start | bytes 2359304 | tf_op jit(solution)/shard_map/ppermute | solution.py:48
  98.0 39.2 %collective-permute-start.31 = (bf16[128,4096]{1,0:T(8,128)(2,1)S(1)}, bf16[128,4096]{1,0:T(8,128)(2,1)S(1)}, u32[]{:S(2)}, u32[]{:S(2)}) collective-permute-start(bf16[128,4096]{1,0:T(8,128)(2,1)S(1)} %constant_dynamic-update-slice_fusion.13.refs_2_.refs_13_), channel_id=1, source_target_pairs={{0,1},{1,0},{2,3},{3,2},{4,5},{5,4},{6,7},{7,6},{8,9},{9,8},{10,11... | collective-permute-start | bytes 3145736 | tf_op jit(solution)/shard_map/ppermute | solution.py:48
  101.1 43.5 %collective-permute-start.39 = (bf16[512,1024]{1,0:T(8,128)(2,1)S(1)}, bf16[512,1024]{1,0:T(8,128)(2,1)}, u32[]{:S(2)}, u32[]{:S(2)}) collective-permute-start(bf16[512,1024]{1,0:T(8,128)(2,1)S(1)} %constant_dynamic-update-slice_fusion.17.refs_4_.refs_5_), channel_id=1, source_target_pairs={{0,4},{1,5},{2,6},{3,7},{4,0},{5,1},{6,2},{7,3},{8,12},{9,13},{10,... | collective-permute-start | bytes 3145736 | tf_op jit(solution)/shard_map/ppermute | solution.py:48
  137.3 28.9 %collective-permute-start.30 = (bf16[128,4096]{1,0:T(8,128)(2,1)S(1)}, bf16[128,4096]{1,0:T(8,128)(2,1)}, u32[]{:S(2)}, u32[]{:S(2)}) collective-permute-start(bf16[128,4096]{1,0:T(8,128)(2,1)S(1)} %collective-permute-done.28.refs_3_.refs_14_), channel_id=1, source_target_pairs={{0,4},{1,5},{2,6},{3,7},{4,0},{5,1},{6,2},{7,3},{8,12},{9,13},{10,... | collective-permute-start | bytes 3145736 | tf_op jit(solution)/shard_map/ppermute | solution.py:48
  139.0 40.1 %collective-permute-start.38 = (bf16[512,1024]{1,0:T(8,128)(2,1)S(1)}, bf16[512,1024]{1,0:T(8,128)(2,1)}, u32[]{:S(2)}, u32[]{:S(2)}) collective-permute-start(bf16[512,1024]{1,0:T(8,128)(2,1)S(1)} %constant_dynamic-update-slice_fusion.17.refs_4_.refs_5_), channel_id=1, source_target_pairs={{0,2},{1,3},{2,0},{3,1},{4,6},{5,7},{6,4},{7,5},{8,10},{9,11},{10,... | collective-permute-start | bytes 3145736 | tf_op jit(solution)/shard_map/ppermute | solution.py:48
  139.5 40.2 %collective-permute-start.32 = (bf16[128,4096]{1,0:T(8,128)(2,1)S(1)}, bf16[128,4096]{1,0:T(8,128)(2,1)}, u32[]{:S(2)}, u32[]{:S(2)}) collective-permute-start(bf16[128,4096]{1,0:T(8,128)(2,1)S(1)} %collective-permute-done.28.refs_3_.refs_14_), channel_id=1, source_target_pairs={{0,1},{1,0},{2,3},{3,2},{4,5},{5,4},{6,7},{7,6},{8,9},{9,8},{10,11... | collective-permute-start | bytes 3145736 | tf_op jit(solution)/shard_map/ppermute | solution.py:48
  144.6 35.2 %collective-permute-start.33 = (bf16[128,4096]{1,0:T(8,128)(2,1)}, bf16[128,4096]{1,0:T(8,128)(2,1)}, u32[]{:S(2)}, u32[]{:S(2)}) collective-permute-start(bf16[128,4096]{1,0:T(8,128)(2,1)} %collective-permute-done.29.refs_4_.refs_15_), channel_id=1, source_target_pairs={{0,1},{1,0},{2,3},{3,2},{4,5},{5,4},{6,7},{7,6},{8,9},{9,8},{10,11... | collective-permute-start | bytes 3145736 | tf_op jit(solution)/shard_map/ppermute | solution.py:48
  144.6 42.2 %collective-permute-start.40 = (bf16[512,1024]{1,0:T(8,128)(2,1)}, bf16[512,1024]{1,0:T(8,128)(2,1)}, u32[]{:S(2)}, u32[]{:S(2)}) collective-permute-start(bf16[512,1024]{1,0:T(8,128)(2,1)} %collective-permute-done.39.refs_6_.refs_7_), channel_id=1, source_target_pairs={{0,2},{1,3},{2,0},{3,1},{4,6},{5,7},{6,4},{7,5},{8,10},{9,11},{10,... | collective-permute-start | bytes 3145736 | tf_op jit(solution)/shard_map/ppermute | solution.py:48
  166.2 53.4 %collective-permute-start.34 = (bf16[128,4096]{1,0:T(8,128)(2,1)}, bf16[128,4096]{1,0:T(8,128)(2,1)}, u32[]{:S(2)}, u32[]{:S(2)}) collective-permute-start(bf16[128,4096]{1,0:T(8,128)(2,1)} %collective-permute-done.30.refs_5_.refs_16_), channel_id=1, source_target_pairs={{0,1},{1,0},{2,3},{3,2},{4,5},{5,4},{6,7},{7,6},{8,9},{9,8},{10,11... | collective-permute-start | bytes 3145736 | tf_op jit(solution)/shard_map/ppermute | solution.py:48
  179.1 69.8 %collective-permute-start.41 = (bf16[512,1024]{1,0:T(8,128)(2,1)S(1)}, bf16[512,1024]{1,0:T(8,128)(2,1)S(1)}, u32[]{:S(2)}, u32[]{:S(2)}) collective-permute-start(bf16[512,1024]{1,0:T(8,128)(2,1)S(1)} %constant_dynamic-update-slice_fusion.17.refs_4_.refs_5_), channel_id=1, source_target_pairs={{0,1},{1,0},{2,3},{3,2},{4,5},{5,4},{6,7},{7,6},{8,9},{9,8},{10,11... | collective-permute-start | bytes 3145736 | tf_op jit(solution)/shard_map/ppermute | solution.py:48
  179.7 69.2 %collective-permute-start.43 = (bf16[512,1024]{1,0:T(8,128)(2,1)}, bf16[512,1024]{1,0:T(8,128)(2,1)S(1)}, u32[]{:S(2)}, u32[]{:S(2)}) collective-permute-start(bf16[512,1024]{1,0:T(8,128)(2,1)} %collective-permute-done.39.refs_6_.refs_7_), channel_id=1, source_target_pairs={{0,1},{1,0},{2,3},{3,2},{4,5},{5,4},{6,7},{7,6},{8,9},{9,8},{10,11... | collective-permute-start | bytes 3145736 | tf_op jit(solution)/shard_map/ppermute | solution.py:48
  179.8 69.1 %collective-permute-start.42 = (bf16[512,1024]{1,0:T(8,128)(2,1)}, bf16[512,1024]{1,0:T(8,128)(2,1)}, u32[]{:S(2)}, u32[]{:S(2)}) collective-permute-start(bf16[512,1024]{1,0:T(8,128)(2,1)} %collective-permute-done.38.refs_5_.refs_6_), channel_id=1, source_target_pairs={{0,1},{1,0},{2,3},{3,2},{4,5},{5,4},{6,7},{7,6},{8,9},{9,8},{10,11... | collective-permute-start | bytes 3145736 | tf_op jit(solution)/shard_map/ppermute | solution.py:48
  186.8 62.1 %collective-permute-start.44 = (bf16[512,1024]{1,0:T(8,128)(2,1)}, bf16[512,1024]{1,0:T(8,128)(2,1)}, u32[]{:S(2)}, u32[]{:S(2)}) collective-permute-start(bf16[512,1024]{1,0:T(8,128)(2,1)} %collective-permute-done.40.refs_7_.refs_8_), channel_id=1, source_target_pairs={{0,1},{1,0},{2,3},{3,2},{4,5},{5,4},{6,7},{7,6},{8,9},{9,8},{10,11... | collective-permute-start | bytes 3145736 | tf_op jit(solution)/shard_map/ppermute | solution.py:48
  289.3 181.7 %collective-permute-start.76 = (bf16[4,4,128,1024]{3,2,1,0:T(8,128)(2,1)}, bf16[4,4,128,1024]{3,2,1,0:T(8,128)(2,1)}, u32[]{:S(2)}, u32[]{:S(2)}) collective-permute-start(bf16[4,4,128,1024]{3,2,1,0:T(8,128)(2,1)} %get-tuple-element.72), channel_id=1, source_target_pairs={{0,1},{1,0},{2,3},{3,2},{4,5},{5,4},{6,7},{7,6},{8,9},{9,8},{10,11... | collective-permute-start | bytes 12582920 | tf_op jit(solution)/shard_map/ppermute | solution.py:48
  373.7 71.8 %collective-permute-start.45 = (bf16[4,4,96,1024]{3,2,1,0:T(8,128)(2,1)}, bf16[4,4,96,1024]{3,2,1,0:T(8,128)(2,1)}, u32[]{:S(2)}, u32[]{:S(2)}) collective-permute-start(bf16[4,4,96,1024]{3,2,1,0:T(8,128)(2,1)} %get-tuple-element.61), channel_id=1, source_target_pairs={{0,1},{1,0},{2,3},{3,2},{4,5},{5,4},{6,7},{7,6},{8,9},{9,8},{10,11... | collective-permute-start | bytes 9437192 | tf_op jit(solution)/shard_map/ppermute | solution.py:48
  398.2 76.2 %collective-permute-start.69 = (bf16[4,4,32,4096]{3,2,1,0:T(8,128)(2,1)}, bf16[4,4,32,4096]{3,2,1,0:T(8,128)(2,1)}, u32[]{:S(2)}, u32[]{:S(2)}) collective-permute-start(bf16[4,4,32,4096]{3,2,1,0:T(8,128)(2,1)} %get-tuple-element.70), channel_id=1, source_target_pairs={{0,1},{1,0},{2,3},{3,2},{4,5},{5,4},{6,7},{7,6},{8,9},{9,8},{10,11... | collective-permute-start | bytes 12582920 | tf_op jit(solution)/shard_map/ppermute | solution.py:48
  474.4 36.5 %collective-permute-start.78 = (bf16[4,128,1024]{2,1,0:T(8,128)(2,1)S(1)}, bf16[4,128,1024]{2,1,0:T(8,128)(2,1)S(1)}, u32[]{:S(2)}, u32[]{:S(2)}) collective-permute-start(bf16[4,128,1024]{2,1,0:T(8,128)(2,1)S(1)} %get-tuple-element.82), channel_id=1, source_target_pairs={{0,2},{1,3},{2,0},{3,1},{4,6},{5,7},{6,4},{7,5},{8,10},{9,11},{10,... | collective-permute-start | bytes 3145736 | tf_op jit(solution)/shard_map/ppermute | solution.py:48
  477.4 38.5 %collective-permute-start.70 = (bf16[4,32,4096]{2,1,0:T(8,128)(2,1)S(1)}, bf16[4,32,4096]{2,1,0:T(8,128)(2,1)S(1)}, u32[]{:S(2)}, u32[]{:S(2)}) collective-permute-start(bf16[4,32,4096]{2,1,0:T(8,128)(2,1)S(1)} %get-tuple-element.83), channel_id=1, source_target_pairs={{0,4},{1,5},{2,6},{3,7},{4,0},{5,1},{6,2},{7,3},{8,12},{9,13},{10,... | collective-permute-start | bytes 3145736 | tf_op jit(solution)/shard_map/ppermute | solution.py:48
  480.0 34.0 %collective-permute-start.61 = (bf16[32,1024]{1,0:T(8,128)(2,1)S(1)}, bf16[32,1024]{1,0:T(8,128)(2,1)S(1)}, u32[]{:S(2)}, u32[]{:S(2)}) collective-permute-start(bf16[32,1024]{1,0:T(8,128)(2,1)S(1)} %get-tuple-element.90), channel_id=1, source_target_pairs={{0,8},{1,9},{2,10},{3,11},{4,12},{5,13},{6,14},{7,15},{8,0},{9,1},... | collective-permute-start | bytes 196616 | tf_op jit(solution)/shard_map/ppermute | solution.py:48
  518.2 43.2 %collective-permute-start.72 = (bf16[4,32,4096]{2,1,0:T(8,128)(2,1)S(1)}, bf16[4,32,4096]{2,1,0:T(8,128)(2,1)S(1)}, u32[]{:S(2)}, u32[]{:S(2)}) collective-permute-start(bf16[4,32,4096]{2,1,0:T(8,128)(2,1)S(1)} %get-tuple-element.84), channel_id=1, source_target_pairs={{0,4},{1,5},{2,6},{3,7},{4,0},{5,1},{6,2},{7,3},{8,12},{9,13},{10,... | collective-permute-start | bytes 3145736 | tf_op jit(solution)/shard_map/ppermute | solution.py:48
  521.6 39.8 %collective-permute-start.71 = (bf16[4,32,4096]{2,1,0:T(8,128)(2,1)S(1)}, bf16[4,32,4096]{2,1,0:T(8,128)(2,1)S(1)}, u32[]{:S(2)}, u32[]{:S(2)}) collective-permute-start(bf16[4,32,4096]{2,1,0:T(8,128)(2,1)S(1)} %fusion.1), channel_id=1, source_target_pairs={{0,2},{1,3},{2,0},{3,1},{4,6},{5,7},{6,4},{7,5},{8,10},{9,11},{10,... | collective-permute-start | bytes 3145736 | tf_op jit(solution)/shard_map/ppermute | solution.py:48
  (90 other events, 1766.7 us)

commit v2 on v1

v2 whole, which is shorter than its diff:
```python
import math

import jax
import jax.numpy as jnp
from jax import lax
from jax.experimental import pallas as pl
from jax.experimental.pallas import tpu as pltpu
from jax.sharding import PartitionSpec as P

HEADS = 16
DHEAD = 64
EPSILON = 1e-05
MASKED = -1e30
SCALE = DHEAD ** (-0.5)
F32 = jnp.float32
BF16 = jnp.bfloat16
BLOCK = 256
TALL = 256
SUB = 128
SPARE = 10 * 1024 * 1024
ROOM = 60 * 1024 * 1024
PIECES = pl.ANY
SIDES = (0, 2, 4, 6)


def dot(left, right):
    return jnp.dot(left, right, preferred_element_type=F32)


def dot_nt(left, right):
    return lax.dot_general(left, right, (((1,), (1,)), ((), ())), preferred_element_type=F32)


def dot_tn(left, right):
    return lax.dot_general(left, right, (((0,), (0,)), ((), ())), preferred_element_type=F32)


def normalize(rows):
    centred = rows - jnp.mean(rows, axis=-1, keepdims=True)
    factor = lax.rsqrt(jnp.mean(centred * centred, axis=-1, keepdims=True) + EPSILON)
    return centred * factor, factor


def norm_back(grad, normed, factor):
    mean_one = jnp.mean(grad, axis=-1, keepdims=True)
    mean_two = jnp.mean(grad * normed, axis=-1, keepdims=True)
    return factor * (grad - mean_one - normed * mean_two)


def flip(array, bits):
    n = lax.axis_size("fsdp")
    return lax.ppermute(array, "fsdp", [(i, i ^ bits) for i in range(n)])


def hold(*values):
    return lax.optimization_barrier(values)


class Weight:
    def __init__(self, pieces, slot, offset, count, rows, columns, first=0):
        self.pieces, self.slot, self.offset, self.count = pieces, slot, offset, count
        self.rows, self.columns, self.first = rows, columns, first


def gather_line(shard):
    n = lax.axis_size("fsdp")
    return [flip(shard, 8 * k) for k in range(1, n // 8)]


def gather_sides(line):
    return flip(line, 2), flip(line, 4)


def gather_across(beside, above):
    half = beside.shape[0] // 2
    return flip(above[:half], 2), flip(beside[half:], 4)


def start_load(weight, refs, target, here, sem, chunks=0):
    if len(refs) == 1:
        tall = weight.rows // max(chunks, 1)
        columns = pl.ds(weight.first, weight.columns)
        for i in range(max(chunks, 1)):
            some = pl.ds(i * tall, tall)
            pltpu.make_async_copy(
                refs[0].at[some, columns], target.at[some], sem.at[i] if chunks else sem
            ).start()
        return
    count = weight.count
    places = weight.rows // count // 8
    spots = [(side, range(places)) for side in SIDES[:3]]
    spots += [(SIDES[3], range(places // 2)), (SIDES[3], range(places // 2, places))]
    spots += [(side ^ 1, which) for side, which in spots]
    for (low, which), ref in zip(spots, refs):
        for position, k in enumerate(which):
            owner = here ^ (low ^ (8 * k))
            pltpu.make_async_copy(
                ref.at[pl.ds(position * weight.slot + weight.offset, count)],
                target.at[pl.ds(pl.multiple_of(owner * count, count), count)],
                sem.at[(owner >> 3) * chunks // places] if chunks else sem,
            ).start()


def chunk_rows(weight, chunks):
    tall = weight.rows // chunks
    return [pl.ds(i * tall, tall) for i in range(chunks)]


def wait_load(target, sem):
    pltpu.make_async_copy(target, target, sem).wait()


def sum_everywhere(array):
    n = lax.axis_size("fsdp")
    bit = 1
    while bit < n:
        array = array + flip(array, bit)
        bit *= 2
    return array


def sum_round(array, flips):
    return sum([flip(array, bits) for bits in flips], array)


def add_low(*arrays):
    total = arrays[0].astype(F32)
    for array in arrays[1:]:
        total = total + array.astype(F32)
    return total


def low_sum(*arrays):
    return add_low(*arrays).astype(BF16)


def sides_of(keep, got):
    half = max(keep.shape[1] // 2, 1)
    parts = ((3, 0), (3, half), (1, 0), (2, half), (1, half), (2, 0))
    return [low_sum(keep[s, p : p + half], got[s, p : p + half]) for s, p in parts]


def flip_first(sides):
    return flip(sides[0], 2), flip(sides[1], 4), flip(sides[2], 2), flip(sides[3], 4)


def flip_second(sides, first):
    return flip(low_sum(sides[4], first[1]), 2), flip(low_sum(sides[5], first[0]), 4)


def flip_diagonal(keep, got):
    half = max(keep.shape[1] // 2, 1)
    low = lambda p: low_sum(keep[3, p : p + half], got[3, p : p + half])
    return flip(low(0), 2), flip(low(half), 4)


def flip_whole(keep, got, moved):
    half = max(keep.shape[1] // 2, 1)
    beside = [low_sum(keep[1, :half], got[1, :half]), low_sum(keep[1, half:], got[1, half:], moved[1])]
    above = [low_sum(keep[2, :half], got[2, :half], moved[0]), low_sum(keep[2, half:], got[2, half:])]
    beside, above = flip(jnp.concatenate(beside), 2), flip(jnp.concatenate(above), 4)
    return (None, None, beside[:half], above[half:]), (beside[half:], above[:half])


def flip_line(keep, got, first, second):
    places = keep.shape[1]
    half = max(places // 2, 1)
    pieces = []
    for k in range(places):
        pair = (first[2][k], second[1][k]) if k < half else (second[0][k - half], first[3][k - half])
        pieces.append(add_low(keep[0, k], got[0, k], *pair))
    arrived = [flip(pieces[k].astype(BF16), 8 * k) for k in range(1, places)]
    return pieces[0], arrived


def operands_of(weights):
    arrays, where = [], []
    for weight in weights:
        places = []
        for piece in weight.pieces:
            for position, array in enumerate(arrays):
                if array is piece:
                    places.append(position)
                    break
            else:
                places.append(len(arrays))
                arrays.append(piece)
        where.append(places)
    return arrays, where


def call(body, grid, info, inputs, specs, weights, outs, out_specs, scratch, flops, name, exps=0, aliases={}):
    arrays, where = operands_of(weights)
    count = len(inputs)

    def kernel(info_ref, *refs):
        ins = refs[:count]
        pieces = refs[count : count + len(arrays)]
        held = [[pieces[p] for p in places] for places in where]
        body(info_ref, ins, held, refs[count + len(arrays) :])

    room = SPARE
    flat = list(zip(specs, inputs)) + list(zip(jax.tree.leaves(out_specs), jax.tree.leaves(outs)))
    for spec, array in flat:
        if spec.block_shape is not None:
            room += 2 * math.prod(spec.block_shape) * array.dtype.itemsize
    for held in scratch:
        if getattr(held, "shape", None) and held.dtype in (F32, BF16):
            room += math.prod(held.shape) * held.dtype.itemsize
    moved = sum(a.size * a.dtype.itemsize for a in list(inputs) + arrays)
    moved += sum(o.size * o.dtype.itemsize for o in jax.tree.leaves(outs))
    return pl.pallas_call(
        kernel,
        grid_spec=pltpu.PrefetchScalarGridSpec(
            num_scalar_prefetch=1,
            grid=grid,
            in_specs=list(specs) + [pl.BlockSpec(memory_space=PIECES)] * len(arrays),
            out_specs=out_specs,
            scratch_shapes=scratch,
        ),
        out_shape=outs,
        compiler_params=pltpu.CompilerParams(
            vmem_limit_bytes=max(room, ROOM), dimension_semantics=("arbitrary",) * len(grid)
        ),
        cost_estimate=pl.CostEstimate(flops=flops, bytes_accessed=moved, transcendentals=exps),
        input_output_aliases=aliases,
        name=name,
    )(info, *inputs, *arrays)


def shape_of(shape, dtype):
    return jax.ShapeDtypeStruct(shape, dtype)


def whole(shape):
    return pl.BlockSpec(shape, lambda *_: (0,) * len(shape))


def sub_blocks(rows):
    return [slice(start, start + SUB) for start in range(0, rows, SUB)]


def by_rows(columns, rows=BLOCK):
    return pl.BlockSpec((rows, columns), lambda i, *_: (i, 0))


def stacked(arrays, columns):
    rows = [array.shape[0] for array in arrays for _ in range(array.shape[1] // columns)]

    def kernel(*refs):
        out_ref, start = refs[-1], 0
        for ref in refs[:-1]:
            for first in range(0, ref.shape[1], columns):
                out_ref[start : start + ref.shape[0], :] = ref[:, first : first + columns]
                start += ref.shape[0]

    return pl.pallas_call(
        kernel,
        out_shape=shape_of((sum(rows), columns), arrays[0].dtype),
        name="stacked",
    )(*arrays)


def project_qkv(info, tokens, biases, weights):
    rows, width = tokens.shape

    def body(info_ref, ins, held, rest):
        tokens_ref, bias_ref = ins
        out_ref, matrix, sem = rest
        which = pl.program_id(0)

        @pl.when(which == 0)
        def _():
            for i, weight in enumerate(weights):
                start_load(weight, held[i], matrix.at[i], info_ref[0], sem.at[i])

        wait_load(matrix.at[which], sem.at[which])
        factor = jnp.where(which == 0, SCALE, 1.0).astype(F32)
        for start in range(0, rows, BLOCK):
            part = pl.ds(start, BLOCK)
            total = dot(tokens_ref[part, :], matrix[which]) + bias_ref[0]
            out_ref[0, part, :] = (total * factor).astype(BF16)

    return call(
        body,
        (3,),
        info,
        (tokens, biases),
        (whole(tokens.shape), pl.BlockSpec((1, 1, width), lambda i, *_: (i, 0, 0))),
        weights,
        shape_of((3, rows, width), BF16),
        pl.BlockSpec((1, rows, width), lambda i, *_: (i, 0, 0)),
        [pltpu.VMEM((3, width, width), BF16), pltpu.SemaphoreType.DMA((3,))],
        6 * rows * width * width,
        "project_qkv",
    )


def head_masks(span, length):
    lane = lax.broadcasted_iota(jnp.int32, (span, 2 * DHEAD), 1)
    place = lax.broadcasted_iota(jnp.int32, (span, 2 * DHEAD), 0)
    return lane, jnp.where(place < length, 0.0, MASKED).astype(F32)


def marked(array, lane, head, mark):
    own = lane // DHEAD == head
    spare = lane == (1 - head) * DHEAD
    return jnp.where(own, array.astype(F32), jnp.where(spare, mark, 0.0)).astype(BF16)


def attend(info, qkv, seqs, which, before):
    _, rows, width = qkv.shape
    span = rows // seqs
    pairs = width // (2 * DHEAD)

    def body(info_ref, ins, held, rest):
        query_ref, key_ref, value_ref = ins[:3]
        mixed_ref, logsum_ref = rest
        length = info_ref[1 + which]
        lane, mark = head_masks(span, length)
        query, keys = query_ref[0], key_ref[0]
        value_t = value_ref[0].T
        mixed = []
        for head in range(2):
            key_one = marked(keys, lane, head, mark)
            query_one = marked(query, lane, head, 1.0)
            scores = dot_nt(key_one, query_one)
            top = jnp.max(scores, axis=0, keepdims=True)
            expo = jnp.exp(scores - top)
            total = jnp.sum(expo, axis=0, keepdims=True)
            out = dot(value_t[head * DHEAD : (head + 1) * DHEAD], expo.astype(BF16))
            mixed.append(out / total)
            logsum_ref[0, 0, head : head + 1, :] = top + jnp.log(total)
        mixed_ref[...] = jnp.concatenate(mixed, axis=0).T.astype(BF16)

    def block(part):
        return pl.BlockSpec((1, span, 2 * DHEAD), lambda p, *_: (part, which, p))

    return call(
        body,
        (pairs,),
        info,
        (qkv, qkv, qkv) + before,
        [block(i) for i in range(3)] + [pl.BlockSpec(memory_space=pl.ANY)] * len(before),
        [],
        (shape_of((rows, width), BF16), shape_of((seqs, pairs, 8, span), F32)),
        (
            pl.BlockSpec((span, 2 * DHEAD), lambda p, *_: (which, p)),
            pl.BlockSpec((1, 1, 8, span), lambda p, *_: (which, p, 0, 0)),
        ),
        [],
        8 * span * span * width,
        "attend",
        exps=span * span * HEADS,
        aliases={4: 0, 5: 1} if before else {},
    )


def attend_back(info, qkv, grad_mixed, logsum, seqs, which, steps):
    _, rows, width = qkv.shape
    span = rows // seqs
    pairs = width // (2 * DHEAD)

    def body(info_ref, ins, held, rest):
        query_ref, key_ref, value_ref, grad_ref, logsum_ref = ins[:5]
        step_ref, sums_ref = rest
        length = info_ref[1 + which]
        lane, mark = head_masks(span, length)
        query, keys, values, grad = query_ref[0], key_ref[0], value_ref[0], grad_ref[...]
        key_t = keys.T
        query_steps, key_steps, value_steps = [], [], []
        for head in range(2):
            key_one = marked(keys, lane, head, mark)
            query_one = marked(query, lane, head, 1.0)
            value_one = marked(values, lane, head, 0.0)
            scores = dot_nt(key_one, query_one)
            probs = jnp.exp(scores - logsum_ref[0, 0, head : head + 1, :])
            grad_probs = dot_nt(value_one, grad)
            value_steps.append(dot(probs.astype(BF16), grad))
            inner = jnp.sum(grad_probs * probs, axis=0, keepdims=True)
            grad_scores = (probs * (grad_probs - inner)).astype(BF16)
            key_steps.append(dot(grad_scores, query))
            query_steps.append(
                dot(key_t[head * DHEAD : (head + 1) * DHEAD], grad_scores) * SCALE
            )
        first = lane < DHEAD
        query_step = jnp.concatenate(query_steps, axis=0).T.astype(BF16)
        key_step = jnp.where(first, key_steps[0], key_steps[1]).astype(BF16)
        value_step = jnp.where(first, value_steps[0], value_steps[1]).astype(BF16)
        step_ref[0] = query_step
        step_ref[1] = key_step
        step_ref[2] = value_step
        sums_ref[0:1, :] = jnp.sum(query_step.astype(F32), axis=0, keepdims=True)
        sums_ref[1:2, :] = jnp.sum(value_step.astype(F32), axis=0, keepdims=True)

    def block(part):
        return pl.BlockSpec((1, span, 2 * DHEAD), lambda p, *_: (part, which, p))

    return call(
        body,
        (pairs,),
        info,
        (qkv, qkv, qkv, grad_mixed, logsum) + (() if steps is None else (steps,)),
        [block(i) for i in range(3)]
        + [
            pl.BlockSpec((span, 2 * DHEAD), lambda p, *_: (which, p)),
            pl.BlockSpec((1, 1, 8, span), lambda p, *_: (which, p, 0, 0)),
        ]
        + ([] if steps is None else [pl.BlockSpec(memory_space=pl.ANY)]),
        [],
        (shape_of((3, rows, width), BF16), shape_of((8, width), F32)),
        (
            pl.BlockSpec((3, span, 2 * DHEAD), lambda p, *_: (0, which, p)),
            pl.BlockSpec((8, 2 * DHEAD), lambda p, *_: (0, p)),
        ),
        [],
        10 * span * span * width * 2,
        "attend_back",
        exps=span * span * HEADS,
        aliases={} if steps is None else {6: 0},
    )


def project_out(info, mixed, tokens, vectors, weight):
    rows, width = tokens.shape

    def body(info_ref, ins, held, rest):
        mixed_ref, tokens_ref, vector_ref = ins
        normed_ref, low_ref, factor_ref, matrix, sem = rest

        @pl.when(pl.program_id(0) == 0)
        def _():
            start_load(weight, held[0], matrix, info_ref[0], sem)
            wait_load(matrix, sem)

        for part in sub_blocks(TALL):
            branch = dot(mixed_ref[part, :], matrix[...]) + vector_ref[2:3, :]
            normed, factor = normalize(tokens_ref[part, :].astype(F32) + branch)
            normed_ref[part, :] = normed.astype(BF16)
            low_ref[part, :] = (normed * vector_ref[3:4, :] + vector_ref[4:5, :]).astype(BF16)
            factor_ref[part, :] = jnp.broadcast_to(factor, (SUB, 128))

    return call(
        body,
        (rows // TALL,),
        info,
        (mixed, tokens, vectors),
        (by_rows(width, TALL), by_rows(width, TALL), whole(vectors.shape)),
        [weight],
        (shape_of((rows, width), BF16), shape_of((rows, width), BF16), shape_of((rows, 128), F32)),
        (by_rows(width, TALL), by_rows(width, TALL), by_rows(128, TALL)),
        [pltpu.VMEM((width, width), BF16), pltpu.SemaphoreType.DMA],
        2 * rows * width * width,
        "project_out",
    )


def gelu_both(hidden):
    share = 0.5 * lax.erf(hidden * 0.7071067811865476) + 0.5
    bell = jnp.exp(-0.5 * (hidden * hidden))
    return hidden * share, share + hidden * (bell * 0.3989422804014327)


def feed_in(info, low, bias, weights, begin, end, before):
    rows, width = low.shape
    part = weights[0].columns
    wide = len(weights) * part
    steps = end - begin

    def body(info_ref, ins, held, rest):
        low_ref, bias_ref = ins[:2]
        active_ref, slope_ref, matrix, sem = rest
        step = pl.program_id(0)

        @pl.when(step == 0)
        def _():
            for i in range(steps):
                start_load(weights[begin + i], held[i], matrix.at[i], info_ref[0], sem.at[i])

        wait_load(matrix.at[step], sem.at[step])
        for start in range(0, rows, BLOCK):
            some = pl.ds(start, BLOCK)
            hidden = dot(low_ref[some, :], matrix[step]) + bias_ref[...]
            active, slope = gelu_both(hidden)
            active_ref[some, :] = active.astype(BF16)
            slope_ref[some, :] = slope.astype(BF16)

    columns = pl.BlockSpec((rows, part), lambda i, *_: (0, begin + i))
    return call(
        body,
        (steps,),
        info,
        (low, bias) + before,
        (whole(low.shape), pl.BlockSpec((1, part), lambda i, *_: (0, begin + i)))
        + (pl.BlockSpec(memory_space=pl.ANY),) * len(before),
        weights[begin:end],
        (shape_of((rows, wide), BF16), shape_of((rows, wide), BF16)),
        (columns, columns),
        [pltpu.VMEM((steps, width, part), BF16), pltpu.SemaphoreType.DMA((steps,))],
        2 * rows * width * part * steps,
        "feed_in",
        exps=rows * part * steps,
        aliases={3: 0, 4: 1} if before else {},
    )


def feed_out(info, active, normed, cotangent, vectors, weight, span):
    rows, wide = active.shape
    width = weight.columns

    def body(info_ref, ins, held, rest):
        active_ref, normed_ref, cotangent_ref, vector_ref = ins
        out_ref, branch_ref, sums_ref, matrix, sem = rest
        step = pl.program_id(0)

        @pl.when(step == 0)
        def _():
            start_load(weight, held[0], matrix, info_ref[0], sem, chunks=2)
            sums_ref[...] = jnp.zeros_like(sums_ref)

        total = 0.0
        for i, some in enumerate(chunk_rows(weight, 2)):

            @pl.when(step == 0)
            def _():
                wait_load(matrix.at[some], sem.at[i])

            total += dot(active_ref[:, some], matrix[some, :])
        sequence = (step * TALL) // span
        length = info_ref[1 + sequence]
        for part in sub_blocks(TALL):
            middle = normed_ref[part, :].astype(F32) * vector_ref[3:4, :] + vector_ref[4:5, :]
            branch = total[part, :] + vector_ref[5:6, :]
            second, factor = normalize(middle + branch)
            gain = vector_ref[6:7, :]
            out_ref[part, :] = (second * gain + vector_ref[7:8, :]).astype(BF16)
            places = step * TALL + part.start + lax.broadcasted_iota(jnp.int32, (SUB, 1), 0)
            valid = places - sequence * span < length
            grad = jnp.where(valid, cotangent_ref[part, :].astype(F32), 0.0)
            sums_ref[0:1, :] += jnp.sum(grad * second, axis=0, keepdims=True)
            sums_ref[1:2, :] += jnp.sum(grad, axis=0, keepdims=True)
            back = norm_back(grad * gain, second, factor)
            branch = back.astype(BF16)
            branch_ref[part, :] = branch
            sums_ref[2:3, :] += jnp.sum(branch.astype(F32), axis=0, keepdims=True)

    return call(
        body,
        (rows // TALL,),
        info,
        (active, normed, cotangent, vectors),
        (by_rows(wide, TALL), by_rows(width, TALL), by_rows(width, TALL), whole(vectors.shape)),
        [weight],
        (
            shape_of((rows, width), BF16),
            shape_of((rows, width), BF16),
            shape_of((8, width), F32),
        ),
        (by_rows(width, TALL), by_rows(width, TALL), whole((8, width))),
        [pltpu.VMEM((wide, width), BF16), pltpu.SemaphoreType.DMA((2,))],
        2 * rows * width * wide,
        "feed_out",
    )


def hidden_back(info, branch, slope, outer):
    rows, width = branch.shape
    wide = slope.shape[1]
    steps = 2
    part = wide // steps

    def body(info_ref, ins, held, rest):
        branch_ref, slope_ref = ins
        hidden_ref, bias_ref, big, sem = rest
        step = pl.program_id(0)

        @pl.when(step == 0)
        def _():
            start_load(outer, held[0], big, info_ref[0], sem, chunks=steps)

        some = pl.ds(pl.multiple_of(step * part, part), part)
        wait_load(big.at[some], sem.at[step])
        total = jnp.zeros((8, part), F32)
        for start in range(0, rows, BLOCK):
            here = slice(start, start + BLOCK)
            grad = dot_nt(branch_ref[here, :], big[some, :]) * slope_ref[here, :].astype(F32)
            grad = grad.astype(BF16)
            hidden_ref[here, :] = grad
            total += jnp.sum(grad.astype(F32).reshape(BLOCK // 8, 8, part), axis=0)
        bias_ref[...] = jnp.broadcast_to(jnp.sum(total, axis=0, keepdims=True), bias_ref.shape)

    columns = pl.BlockSpec((rows, part), lambda i, *_: (0, i))
    return call(
        body,
        (steps,),
        info,
        (branch, slope),
        (whole(branch.shape), columns),
        [outer],
        (shape_of((rows, wide), BF16), shape_of((8, wide), F32)),
        (columns, pl.BlockSpec((8, part), lambda i, *_: (0, i))),
        [pltpu.VMEM((wide, width), BF16), pltpu.SemaphoreType.DMA((steps,))],
        2 * rows * width * wide,
        "hidden_back",
    )


def middle_back(info, branch, hidden, normed, factor, vectors, inner, attn):
    rows, width = branch.shape
    wide = hidden.shape[1]
    chunks, part = len(inner), inner[0].columns

    def body(info_ref, ins, held, rest):
        branch_ref, hidden_ref, normed_ref, factor_ref, vector_ref = ins
        proj_ref, mixed_ref, sums_ref, big, small, sem = rest
        step = pl.program_id(0)

        @pl.when(step == 0)
        def _():
            for i in range(chunks):
                start_load(inner[i], held[i], big.at[i], info_ref[0], sem.at[i])
            start_load(attn, held[chunks], small, info_ref[0], sem.at[chunks])
            sums_ref[...] = jnp.zeros_like(sums_ref)

        middle = branch_ref[...].astype(F32)
        for i in range(chunks):

            @pl.when(step == 0)
            def _():
                wait_load(big.at[i], sem.at[i])

            middle += dot_nt(hidden_ref[:, i * part : (i + 1) * part], big[i])

        @pl.when(step == 0)
        def _():
            wait_load(small, sem.at[chunks])

        normed = normed_ref[...].astype(F32)
        sums_ref[0:1, :] += jnp.sum(middle * normed, axis=0, keepdims=True)
        sums_ref[1:2, :] += jnp.sum(middle, axis=0, keepdims=True)
        first = norm_back(middle * vector_ref[3:4, :], normed, factor_ref[:, 0:1])
        proj = first.astype(BF16)
        proj_ref[...] = proj
        sums_ref[2:3, :] += jnp.sum(proj.astype(F32), axis=0, keepdims=True)
        mixed_ref[...] = dot_nt(proj, small[...]).astype(BF16)

    return call(
        body,
        (rows // BLOCK,),
        info,
        (branch, hidden, normed, factor, vectors),
        (by_rows(width), by_rows(wide), by_rows(width), by_rows(128), whole(vectors.shape)),
        inner + [attn],
        (shape_of((rows, width), BF16), shape_of((rows, width), BF16), shape_of((8, width), F32)),
        (by_rows(width), by_rows(width), whole((8, width))),
        [
            pltpu.VMEM((chunks, width, part), BF16),
            pltpu.VMEM((width, width), BF16),
            pltpu.SemaphoreType.DMA((chunks + 1,)),
        ],
        2 * rows * width * wide + 2 * rows * width * width,
        "middle_back",
    )


def input_back(info, proj, steps, weights):
    rows, width = proj.shape

    def body(info_ref, ins, held, rest):
        proj_ref, step_ref = ins
        out_ref, matrix, sem = rest

        @pl.when(pl.program_id(0) == 0)
        def _():
            for i, weight in enumerate(weights):
                start_load(weight, held[i], matrix.at[i], info_ref[0], sem.at[i])

        total = proj_ref[...].astype(F32)
        for i in range(3):

            @pl.when(pl.program_id(0) == 0)
            def _():
                wait_load(matrix.at[i], sem.at[i])

            total += dot_nt(step_ref[i], matrix[i])
        out_ref[...] = total.astype(BF16)

    return call(
        body,
        (rows // BLOCK,),
        info,
        (proj, steps),
        (by_rows(width), pl.BlockSpec((3, BLOCK, width), lambda i, *_: (0, i, 0))),
        weights,
        shape_of((rows, width), BF16),
        by_rows(width),
        [pltpu.VMEM((3, width, width), BF16), pltpu.SemaphoreType.DMA((3,))],
        6 * rows * width * width,
        "input_back",
    )


def weight_grad(info, lefts, rights, places, name):
    rows, height = lefts[0].shape
    slot = height // (8 * places)
    block = 8 * slot
    part = min(1024, rights[0].shape[-1])
    counts = [r.shape[0] if r.ndim == 3 else r.shape[1] // part for r in rights]
    firsts = [sum(counts[:i]) for i in range(len(counts))]
    parts = sum(counts)
    half = height // 2

    def body(info_ref, ins, held, rest):
        left_refs, right_refs = ins[: len(lefts)], ins[len(lefts) :]
        keep_ref, send_ref, sorted_ref = rest
        here = info_ref[0]
        step = pl.program_id(0)
        for left_ref, right_ref, first, count in zip(left_refs, right_refs, firsts, counts):

            @pl.when(step == first)
            def _():
                for z in range(places):
                    turned = left_ref[:, z * block : (z + 1) * block].T
                    for k in range(8):
                        relative = (z * 8 + k) ^ here
                        spot = (relative & 1) * 4 + ((relative >> 1) & 3)
                        spot = spot * places + (relative >> 3)
                        sorted_ref[pl.ds(pl.multiple_of(spot * slot, slot), slot), :] = turned[
                            k * slot : (k + 1) * slot
                        ]

            @pl.when((step >= first) & (step < first + count))
            def _():
                right = right_ref[0] if len(right_ref.shape) == 3 else right_ref[...]
                for out_ref, start in ((keep_ref, 0), (send_ref, half)):
                    for side in range(4):
                        size = half // 4
                        total = dot(sorted_ref[start + side * size : start + (side + 1) * size, :], right)
                        out_ref[side] = total.astype(BF16).reshape(places, slot, part)

    def right_spec(right, first, count):
        place = lambda w: jnp.clip(w - first, 0, count - 1)
        if right.ndim == 3:
            return pl.BlockSpec((1, rows, part), lambda w, *_: (place(w), 0, 0))
        return pl.BlockSpec((rows, part), lambda w, *_: (0, place(w)))

    out = shape_of((4, places, parts * slot, part), BF16)
    out_block = pl.BlockSpec((4, places, slot, part), lambda w, *_: (0, 0, w, 0))
    return call(
        body,
        (parts,),
        info,
        tuple(lefts) + tuple(rights),
        [whole(left.shape) for left in lefts]
        + [right_spec(r, f, c) for r, f, c in zip(rights, firsts, counts)],
        [],
        (out, out),
        (out_block, out_block),
        [pltpu.VMEM((height, rows), BF16)],
        2 * rows * height * parts * part,
        name,
    )


def weight_grad_tall(info, left, right, places, name):
    rows, height = left.shape
    width = right.shape[1]
    slot = height // (8 * places)

    def body(info_ref, ins, held, rest):
        left_ref, right_ref = ins
        keep_ref, send_ref = rest
        here = info_ref[0]
        for side in range(4):
            for out_ref, other in ((keep_ref, 0), (send_ref, 1)):
                which = (here & 7) ^ (2 * side + other)
                some = pl.ds(pl.multiple_of(which * slot, slot), slot)
                out_ref[side, 0] = dot_tn(left_ref[:, some], right_ref[...]).astype(BF16)

    out = shape_of((4, places, slot, width), BF16)
    block = pl.BlockSpec((4, 1, slot, width), lambda z, *_: (0, z, 0, 0))
    return call(
        body,
        (places,),
        info,
        (left, right),
        (
            pl.BlockSpec((rows, 8 * slot), lambda z, info: (0, z ^ (info[0] >> 3))),
            whole(right.shape),
        ),
        [],
        (out, out),
        (block, block),
        [],
        2 * rows * height * width,
        name,
    )


def sums_of(second, first, attn, wide):
    attn = sum(attn)[:2]
    return jnp.concatenate([second[:3], first[:3], attn, wide[:1].reshape(-1, second.shape[1])])


def per_device(
    tokens,
    lengths,
    cotangent,
    query_weight,
    query_bias,
    key_weight,
    value_weight,
    value_bias,
    attn_weight,
    attn_bias,
    first_gain,
    first_shift,
    inner_weight,
    inner_bias,
    outer_weight,
    outer_bias,
    second_gain,
    second_shift,
):
    n = lax.axis_size("fsdp")
    here = lax.axis_index("fsdp").astype(jnp.int32)
    seqs = lengths.shape[0]
    rows, width = tokens.shape
    wide = inner_weight.shape[1]
    span = rows // seqs
    own = query_weight.shape[0]
    tall = outer_weight.shape[0]
    staged = n in (16, 32) and own % 16 == 0
    info = jnp.concatenate([here[None], lengths])

    full = lambda w: lax.all_gather(w, "fsdp", axis=0, tiled=True)
    whole_weight = lambda w: Weight((w,), 0, 0, w.shape[0] // n, w.shape[0], w.shape[1])

    small = jnp.stack(
        (
            query_bias,
            value_bias,
            attn_bias,
            first_gain,
            first_shift,
            outer_bias,
            second_gain,
            second_shift,
        )
    )
    table = jnp.zeros((8 + wide // width, width), BF16)
    table = lax.dynamic_update_slice(table, small, (0, here * own))
    spot = here * tall
    table = lax.dynamic_update_slice(table, inner_bias[None], (8 + spot // width, spot % width))

    if staged:
        places = n // 8
        one = stacked([query_weight, key_weight, value_weight], width)
        two = stacked([inner_weight, attn_weight], width)
        others = gather_line(one)
        for bits in (1, 2, 4):
            table = sum_round(table, (bits,))
        table, two, *others = hold(table, two, *others)
        line = jnp.concatenate([one, *others])
        beside, above = gather_sides(line)
        cut = 3 * own
        others_top = gather_line(two[:cut])
        line, beside, above, two, *others_top = hold(line, beside, above, two, *others_top)
        others_low = gather_line(two[cut:])
        near = (line, beside, above) + gather_across(beside, above)
        table, two, *near = hold(table, two, *near, *others_low)
        near, others_low = near[:5], near[5:]
        table = sum_round(table, [8 * k for k in range(1, places)])
        pieces = near + [flip(piece, 1) for piece in near]
        line_two = jnp.concatenate([two] + [p for pair in zip(others_top, others_low) for p in pair])
        table, line_two, three, *pieces = hold(table, line_two, outer_weight, *pieces)
        qkv_weights = [Weight(pieces, 3 * own, i * own, own, width, width) for i in range(3)]
    else:
        table = sum_everywhere(table)
        qkv_weights = [whole_weight(full(w)) for w in (query_weight, key_weight, value_weight)]
        outer = whole_weight(full(outer_weight))
    table = table.astype(F32)
    vectors, wide_bias = table[:8], table[8:].reshape(1, wide)
    biases = jnp.stack([vectors[0:1], jnp.zeros((1, width), F32), vectors[1:2]])

    blocks = wide // width
    if staged:
        beside, above = gather_sides(line_two)
        others_three = gather_line(three)
        qkv = project_qkv(info, tokens, biases, qkv_weights)
        result = attend(info, qkv, seqs, 0, ())
        beside, above, *result = hold(beside, above, *others_three, *result)
        others_three, result = result[: places - 1], result[places - 1 :]
        near = (line_two, beside, above) + gather_across(beside, above)
        far = tuple(flip(piece, 1) for piece in near[:3])
        line_three = jnp.concatenate([three, *others_three])
        for which in range(1, seqs):
            result = attend(info, qkv, seqs, which, tuple(result))
        mixed, logsum, line_three, *pieces = hold(*result, line_three, *near, *far)
        beside, above = gather_sides(line_three)
        pieces = pieces + [flip(piece, 1) for piece in pieces[3:5]]
        inner = [Weight(pieces, 5 * own, i * own, own, width, width) for i in range(blocks)]
        attn = Weight(pieces, 5 * own, blocks * own, own, width, width)
        normed, low, factor = project_out(info, mixed, tokens, vectors, attn)
        active, slope = feed_in(info, low, wide_bias, inner, 0, blocks // 2, ())
        line_three, beside, above, active, slope = hold(line_three, beside, above, active, slope)
        near = (line_three, beside, above) + gather_across(beside, above)
        far = tuple(flip(piece, 1) for piece in near[:3])
        active, slope = feed_in(info, low, wide_bias, inner, blocks // 2, blocks, (active, slope))
        active, *pieces = hold(active, *near, *far)
        pieces = pieces + [flip(piece, 1) for piece in pieces[3:5]]
        outer = Weight(pieces, tall, 0, tall, wide, width)
    else:
        attn, inner = whole_weight(full(attn_weight)), full(inner_weight)
        inner = [Weight((inner,), 0, 0, own, width, width, i * width) for i in range(blocks)]
        qkv = project_qkv(info, tokens, biases, qkv_weights)
        result = ()
        for which in range(seqs):
            result = attend(info, qkv, seqs, which, tuple(result))
        mixed, logsum = result
        normed, low, factor = project_out(info, mixed, tokens, vectors, attn)
        active, slope = feed_in(info, low, wide_bias, inner, 0, blocks, ())
    output, branch, sums_second = feed_out(
        info, active, normed, cotangent, vectors, outer, span
    )

    def back_of(hidden):
        return middle_back(info, branch, hidden, normed, factor, vectors, inner, attn)

    def attend_all(grad_mixed):
        steps, sums = None, []
        for which in range(seqs):
            steps, some = attend_back(info, qkv, grad_mixed, logsum, seqs, which, steps)
            sums.append(some)
        return steps, sums

    if staged:
        keep_o, send_o = weight_grad_tall(info, active, branch, places, "grad_outer")
        keep_o, send_o, branch = hold(keep_o, send_o, branch)
        got_o = flip(send_o, 1)
        grad_hidden, sums_wide = hidden_back(info, branch, slope, outer)
        got_o, grad_hidden, sums_wide = hold(got_o, grad_hidden, sums_wide)
        sides_o = sides_of(keep_o, got_o)
        grad_hidden, *sides_o = hold(grad_hidden, *sides_o)
        first_o = flip_first(sides_o)
        grad_proj, grad_mixed, sums_first = back_of(grad_hidden)
        first_o, grad_proj, grad_mixed, sums_first = hold(
            first_o, grad_proj, grad_mixed, sums_first
        )
        second_o = flip_second(sides_o, first_o)
        keep, send = weight_grad(
            info, (low, mixed), (grad_hidden, grad_proj), places, "grad_inner_attn"
        )
        second_o, keep, send, grad_mixed = hold(second_o, keep, send, grad_mixed)
        got = flip(send, 1)
        kept_o, arrived_o = flip_line(keep_o, got_o, first_o, second_o)
        steps, some = attend_back(info, qkv, grad_mixed, logsum, seqs, 0, None)
        sums_attn = [some]
        got, kept_o, arrived_o, steps = hold(got, kept_o, arrived_o, steps)
        sides = sides_of(keep, got)
        outer_wgrad = add_low(kept_o, *arrived_o)
        steps, outer_wgrad, *sides = hold(steps, outer_wgrad, *sides)
        first = flip_first(sides)
        for which in range(1, seqs):
            steps, some = attend_back(info, qkv, grad_mixed, logsum, seqs, which, steps)
            sums_attn.append(some)
        keep_two, send_two = weight_grad(info, (tokens,), (steps,), places, "grad_qkv")
        first, steps, keep_two, send_two, *sums_attn = hold(
            first, steps, keep_two, send_two, *sums_attn
        )
        got_two = flip(send_two, 1)
        sums = sums_of(sums_second, sums_first, sums_attn, sums_wide)
        sums = sum_round(sums, (1,))
        second = flip_second(sides, first)
        input_grad = input_back(info, grad_proj, steps, qkv_weights)
        got_two, sums, second, input_grad = hold(got_two, sums, second, input_grad)
        moved_two = flip_diagonal(keep_two, got_two)
        sums = sum_round(sums, [8 * k for k in range(1, places)])
        sums, keep, *moved_two = hold(sums, keep, *moved_two)
        first_two, second_two = flip_whole(keep_two, got_two, moved_two)
        kept, arrived = flip_line(keep, got, first, second)
        sums, first_two, second_two = hold(sums, first_two, second_two)
        sums = sum_round(sum_round(sums, (2,)), (4,))
        kept_two, arrived_two = flip_line(keep_two, got_two, first_two, second_two)
        both = add_low(kept, *arrived)
        qkv_wgrad = add_low(kept_two, *arrived_two)
        attn_wgrad = both[wide // width * own :]
        inner_wgrad = both[: wide // width * own].reshape(wide // width, own, width)
        inner_wgrad = inner_wgrad.transpose(1, 0, 2).reshape(own, wide)
    else:
        scatter = lambda g: lax.psum_scatter(g, "fsdp", scatter_dimension=0, tiled=True)
        outer_wgrad = scatter(dot_tn(active, branch))
        grad_hidden, sums_wide = hidden_back(info, branch, slope, outer)
        grad_proj, grad_mixed, sums_first = back_of(grad_hidden)
        steps, sums_attn = attend_all(grad_mixed)
        input_grad = input_back(info, grad_proj, steps, qkv_weights)
        inner_wgrad = scatter(dot_tn(low, grad_hidden))
        attn_wgrad = scatter(dot_tn(mixed, grad_proj))
        qkv_wgrad = jnp.concatenate([scatter(dot_tn(tokens, steps[i])) for i in range(3)])
        sums = sum_everywhere(sums_of(sums_second, sums_first, sums_attn, sums_wide))

    mine = lax.dynamic_slice(sums, (0, here * own), (8, own))
    inner_bgrad = lax.dynamic_slice(sums, (8 + spot // width, spot % width), (1, tall))[0]
    return (
        output,
        input_grad,
        qkv_wgrad[:own],
        mine[6],
        qkv_wgrad[own : 2 * own],
        qkv_wgrad[2 * own :],
        mine[7],
        attn_wgrad,
        mine[5],
        mine[3],
        mine[4],
        inner_wgrad,
        inner_bgrad,
        outer_wgrad,
        mine[2],
        mine[0],
        mine[1],
    )


def solution(mesh):
    rows, vector = P("fsdp", None), P("fsdp")
    return jax.shard_map(
        per_device,
        mesh=mesh,
        in_specs=(
            rows,
            vector,
            rows,
            rows,
            vector,
            rows,
            rows,
            vector,
            rows,
            vector,
            vector,
            vector,
            rows,
            vector,
            rows,
            vector,
            vector,
            vector,
        ),
        out_specs=(
            rows,
            rows,
            rows,
            vector,
            rows,
            rows,
            vector,
            rows,
            vector,
            vector,
            vector,
            rows,
            vector,
            rows,
            vector,
            vector,
            vector,
        ),
        check_vma=False,
    )
```

time: 592 us -> 460 us (0.78)
  waiting for transfers between devices: 198 us -> 82.4 us
  starting transfers between devices: 94.7 us -> 81.3 us
    ppermute x83 -> x79, waiting for transfers between devices: 198 us -> 82.4 us  [flip(): return lax.ppermute(array, 'fsdp', [(i, i ^ bits) for i in range(n)])]
    ppermute x83 -> x79, starting transfers between devices: 94.7 us -> 81.3 us  [flip(): return lax.ppermute(array, 'fsdp', [(i, i ^ bits) for i in range(n)])]
    concatenate x6 -> x1, local copies, waits for them, and re-layouts: 8.36 us -> 0.01 us  [per_device(): jnp.concatenate([two] + [p for pair in zip(others_top, others_low) for p...]
    pallas_call x12 -> x15, Pallas kernels: 239 us -> 231 us  [call(): pl.pallas_call(kernel, grid_spec=pltpu.PrefetchScalarGridSpec(num_scalar_...]
    convert_element_type x13 -> x12, other arithmetic: 20.3 us -> 27 us  [the longest x8 19.9 us: low_sum(): return add_low(*arrays).astype(BF16)]
  transfers between devices with their start and end apart: 83 -> 79, of which waited for: 31 -> 29; matrix products, arithmetic and copies ran while one was open for 7% -> 6% of each run, Pallas kernels for 35% -> 43%
where the time goes in v2:
time: 460 us; the launch traced here: 452 us
  Pallas kernels  235 us (51%)
  waiting for transfers between devices  82.4 us (18%)
  starting transfers between devices  81.3 us (18%)
  other arithmetic  36.1 us (8%)
  local copies, waits for them, and re-layouts  15.3 us (3%)
    pallas_call x15, Pallas kernels, call(): pl.pallas_call(kernel, grid_spec=pltpu.PrefetchScalarGridSpec(num_scalar_...  231 us
    ppermute x79, waiting for transfers between devices, flip(): return lax.ppermute(array, 'fsdp', [(i, i ^ bits) for i in range(n)])  82.4 us
    ppermute x79, starting transfers between devices, flip(): return lax.ppermute(array, 'fsdp', [(i, i ^ bits) for i in range(n)])  81.3 us
    convert_element_type x8, other arithmetic, low_sum(): return add_low(*arrays).astype(BF16)  19.9 us
  transfers between devices with their start and end apart: 79, of which 29 were waited for; matrix products, arithmetic and copies ran while one was open for 6% of the time, Pallas kernels for 43%

profile of v2, /device:TPU:0, one launch (start us, length us, event | category | flops | bytes accessed | tf_op | source)
XLA Modules:
  0.0 451.6 jit_solution(26384317416633947)
XLA Ops:
  19.1 5.1 %collective-permute-done.4 = bf16[96,1024]{1,0:T(8,128)(2,1)S(1)} collective-permute-done((bf16[96,1024]{1,0:T(8,128)(2,1)}, bf16[96,1024]{1,0:T(8,128)(2,1)S(1)}, u32[]{:S(2)}, u32[]{:S(2)}) %collective-permute-start.4) | collective-permute-done | bytes 196640 | tf_op jit(solution)/shard_map/ppermute | solution.py:52
  32.7 5.3 %collective-permute-done.10 = bf16[96,1024]{1,0:T(8,128)(2,1)S(1)} collective-permute-done((bf16[96,1024]{1,0:T(8,128)(2,1)S(1)}, bf16[96,1024]{1,0:T(8,128)(2,1)S(1)}, u32[]{:S(2)}, u32[]{:S(2)}) %collective-permute-start.10) | collective-permute-done | bytes 196640 | tf_op jit(solution)/shard_map/ppermute | solution.py:52
  38.0 7.9 %collective-permute-done.9 = bf16[96,1024]{1,0:T(8,128)(2,1)S(1)} collective-permute-done((bf16[96,1024]{1,0:T(8,128)(2,1)S(1)}, bf16[96,1024]{1,0:T(8,128)(2,1)S(1)}, u32[]{:S(2)}, u32[]{:S(2)}) %collective-permute-start.9) | collective-permute-done | bytes 196640 | tf_op jit(solution)/shard_map/ppermute | solution.py:52
  80.0 12.3 %project_qkv.1.refs_0_.refs_1_.refs_2_ = bf16[3,1024,1024]{2,1,0:T(8,128)(2,1)} custom-call(s32[3]{0:T(128)} %pad_add_fusion.info_ref, bf16[1024,1024]{1,0:T(8,128)(2,1)} %refs_0_.7, f32[3,1,1024]{2,1,0:T(1,128)} %pad_maximum_fusion.5.refs_1_, bf16[384,1024]{1,0:T(8,128)(2,1)} %copy-done.8, bf16[384,1024]{1,0:T(8,128)(2,1)} %copy-done.15, ...), custom_call_target="tpu_custom_call" | custom-call | flops 6442450944 | bytes 14692352 | tf_op jit(solution)/shard_map/project_qkv/pallas_call | solution.py:212
  92.3 12.7 %attend.2 = (bf16[1024,1024]{1,0:T(8,128)(2,1)}, f32[2,8,8,512]{3,2,1,0:T(8,128)}) custom-call(s32[3]{0:T(128)} %pad_add_fusion.info_ref, bf16[3,1024,1024]{2,1,0:T(8,128)(2,1)} %project_qkv.1.refs_0_.refs_1_.refs_2_, bf16[3,1024,1024]{2,1,0:T(8,128)(2,1)} %project_qkv.1.refs_0_.refs_1_.refs_2_, bf16[3,1024,1024]{2,1,0:T(8,128)(2,1)} %project_qkv.1.refs_0_.refs_1_.refs_2_), custom_call_target="tpu_custom_call" | custom-call | flops 2147483648 | bytes 21233664 | tf_op jit(solution)/shard_map/attend/pallas_call | solution.py:212
  111.5 12.7 %attend.3 = (bf16[1024,1024]{1,0:T(8,128)(2,1)}, f32[2,8,8,512]{3,2,1,0:T(8,128)}) custom-call(s32[3]{0:T(128)} %pad_add_fusion.info_ref, bf16[3,1024,1024]{2,1,0:T(8,128)(2,1)} %project_qkv.1.refs_0_.refs_1_.refs_2_, bf16[3,1024,1024]{2,1,0:T(8,128)(2,1)} %project_qkv.1.refs_0_.refs_1_.refs_2_, ...), custom_call_target="tpu_custom_call", output_to_operand_aliasing={{0}: (4, {}), {1}: (5, {})} | custom-call | flops 2147483648 | bytes 23592960 | tf_op jit(solution)/shard_map/attend/pallas_call | solution.py:212
  130.9 9.2 %project_out.1 = (bf16[1024,1024]{1,0:T(8,128)(2,1)}, bf16[1024,1024]{1,0:T(8,128)(2,1)}, f32[1024,128]{1,0:T(8,128)}) custom-call(s32[3]{0:T(128)} %pad_add_fusion.info_ref, bf16[1024,1024]{1,0:T(8,128)(2,1)} %get-tuple-element.221.refs_0_.refs_1_, bf16[1024,1024]{1,0:T(8,128)(2,1)} %refs_0_.7, f32[8,1024]{1,0:T(8,128)} %slice.472.refs_2_.refs_3_.refs_4_, ...), custom_call_target="tpu_custom_call" | custom-call | flops 2147483648 | bytes 19431424 | tf_op jit(solution)/shard_map/project_out/pallas_call | solution.py:212
  140.2 14.2 %feed_in.2 = (bf16[1024,4096]{1,0:T(8,128)(2,1)}, bf16[1024,4096]{1,0:T(8,128)(2,1)}) custom-call(s32[3]{0:T(128)} %pad_add_fusion.info_ref, bf16[1024,1024]{1,0:T(8,128)(2,1)} %get-tuple-element.230.refs_0_, f32[1,4096]{1,0:T(1,128)} %bitcast.180, bf16[640,1024]{1,0:T(8,128)(2,1)} %copy-done.2, bf16[640,1024]{1,0:T(8,128)(2,1)} %copy-done.1, ...), custom_call_target="tpu_custom_call" | custom-call | flops 4294967296 | bytes 29376512 | tf_op jit(solution)/shard_map/feed_in/pallas_call | solution.py:212
  158.8 13.8 %feed_in.3 = (bf16[1024,4096]{1,0:T(8,128)(2,1)}, bf16[1024,4096]{1,0:T(8,128)(2,1)}) custom-call(s32[3]{0:T(128)} %pad_add_fusion.info_ref, bf16[1024,1024]{1,0:T(8,128)(2,1)} %get-tuple-element.230.refs_0_, f32[1,4096]{1,0:T(1,128)} %bitcast.181, bf16[1024,4096]{1,0:T(8,128)(2,1)} %get-tuple-element.234.refs_2_, ...), custom_call_target="tpu_custom_call", output_to_operand_aliasing={{0}: (3, {}), {1}: (4, {})} | custom-call | flops 4294967296 | bytes 46153728 | tf_op jit(solution)/shard_map/feed_in/pallas_call | solution.py:212
  176.4 21.7 %feed_out.1 = (bf16[1024,1024]{1,0:T(8,128)(2,1)}, bf16[1024,1024]{1,0:T(8,128)(2,1)}, f32[8,1024]{1,0:T(8,128)}) custom-call(s32[3]{0:T(128)} %pad_add_fusion.info_ref, bf16[1024,4096]{1,0:T(8,128)(2,1)} %get-tuple-element.240.refs_0_, bf16[1024,1024]{1,0:T(8,128)(2,1)} %get-tuple-element.241.refs_1_.refs_2_, bf16[1024,1024]{1,0:T(8,128)(2,1)} %refs_2_.3, ...), custom_call_target="tpu_custom_call" | custom-call | flops 8589934592 | bytes 25231360 | tf_op jit(solution)/shard_map/feed_out/pallas_call | solution.py:212
  198.1 14.8 %grad_outer.1 = (bf16[4,4,128,1024]{3,2,1,0:T(8,128)(2,1)}, bf16[4,4,128,1024]{3,2,1,0:T(8,128)(2,1)}) custom-call(s32[3]{0:T(128)} %pad_add_fusion.info_ref, bf16[1024,4096]{1,0:T(8,128)(2,1)} %get-tuple-element.240.refs_0_, bf16[1024,1024]{1,0:T(8,128)(2,1)} %get-tuple-element.255.refs_1_.refs_0_), custom_call_target="tpu_custom_call" | custom-call | flops 8589934592 | bytes 18874368 | tf_op jit(solution)/shard_map/grad_outer/pallas_call | solution.py:212
  213.1 19.1 %hidden_back.1 = (bf16[1024,4096]{1,0:T(8,128)(2,1)}, f32[8,4096]{1,0:T(8,128)}) custom-call(s32[3]{0:T(128)} %pad_add_fusion.info_ref, bf16[1024,1024]{1,0:T(8,128)(2,1)} %get-tuple-element.255.refs_1_.refs_0_, bf16[1024,4096]{1,0:T(8,128)(2,1)} %get-tuple-element.256.refs_1_, bf16[512,1024]{1,0:T(8,128)(2,1)} %pad_maximum_fusion.refs_4_.refs_2_, ...), custom_call_target="tpu_custom_call" | custom-call | flops 8589934592 | bytes 27394048 | tf_op jit(solution)/shard_map/hidden_back/pallas_call | solution.py:212
  232.2 5.2 %fusion.19 = (bf16[2,128,1024]{2,1,0:T(8,128)(2,1)S(1)}, bf16[2,128,1024]{2,1,0:T(8,128)(2,1)S(1)}, bf16[2,128,1024]{2,1,0:T(8,128)(2,1)S(1)}, bf16[2,128,1024]{...) fusion(bf16[4,4,128,1024]{3,2,1,0:T(8,128)(2,1)} %collective-permute-done.45, ...), kind=kLoop, calls=%fused_computation.53 | loop fusion | flops 6291456 | bytes 9437184 | tf_op jit(solution)/shard_map/convert_element_type | solution.py:134
  241.5 20.5 %middle_back.1 = (bf16[1024,1024]{1,0:T(8,128)(2,1)}, bf16[1024,1024]{1,0:T(8,128)(2,1)}, f32[8,1024]{1,0:T(8,128)}) custom-call(s32[3]{0:T(128)} %pad_add_fusion.info_ref, bf16[1024,1024]{1,0:T(8,128)(2,1)} %get-tuple-element.255.refs_1_.refs_0_, bf16[1024,4096]{1,0:T(8,128)(2,1)} %get-tuple-element.267.refs_1_.refs_2_, ...), custom_call_target="tpu_custom_call" | custom-call | flops 10737418240 | bytes 27852800 | tf_op jit(solution)/shard_map/middle_back/pallas_call | solution.py:212
  265.6 18.9 %grad_inner_attn.1 = (bf16[4,4,160,1024]{3,2,1,0:T(8,128)(2,1)}, bf16[4,4,160,1024]{3,2,1,0:T(8,128)(2,1)}) custom-call(s32[3]{0:T(128)} %pad_add_fusion.info_ref, bf16[1024,1024]{1,0:T(8,128)(2,1)} %get-tuple-element.230.refs_0_, bf16[1024,1024]{1,0:T(8,128)(2,1)} %get-tuple-element.221.refs_0_.refs_1_, ...), custom_call_target="tpu_custom_call" | custom-call | flops 10737418240 | bytes 25165824 | tf_op jit(solution)/shard_map/grad_inner_attn/pallas_call | solution.py:212
  291.8 18.0 %attend_back.2 = (bf16[3,1024,1024]{2,1,0:T(8,128)(2,1)}, f32[8,1024]{1,0:T(8,128)}) custom-call(s32[3]{0:T(128)} %pad_add_fusion.info_ref, bf16[3,1024,1024]{2,1,0:T(8,128)(2,1)} %project_qkv.1.refs_0_.refs_1_.refs_2_, bf16[3,1024,1024]{2,1,0:T(8,128)(2,1)} %project_qkv.1.refs_0_.refs_1_.refs_2_, bf16[3,1024,1024]{2,1,0:T(8,128)(2,1)} %project_qkv.1.refs_0_.refs_1_.refs_2_, ...), custom_call_target="tpu_custom_call" | custom-call | flops 5368709120 | bytes 27557888 | tf_op jit(solution)/shard_map/attend_back/pallas_call | solution.py:212
  313.2 6.4 %fusion.7 = (bf16[2,160,1024]{2,1,0:T(8,128)(2,1)S(1)}, bf16[2,160,1024]{2,1,0:T(8,128)(2,1)S(1)}, bf16[2,160,1024]{2,1,0:T(8,128)(2,1)S(1)}, bf16[2,160,1024]{2...) fusion(bf16[4,4,160,1024]{3,2,1,0:T(8,128)(2,1)} %collective-permute-done.52, ...), kind=kLoop, calls=%fused_computation.33 | loop fusion | flops 7864320 | bytes 11796480 | tf_op jit(solution)/shard_map/convert_element_type | solution.py:134
  324.6 17.8 %attend_back.3 = (bf16[3,1024,1024]{2,1,0:T(8,128)(2,1)}, f32[8,1024]{1,0:T(8,128)}) custom-call(s32[3]{0:T(128)} %pad_add_fusion.info_ref, bf16[3,1024,1024]{2,1,0:T(8,128)(2,1)} %project_qkv.1.refs_0_.refs_1_.refs_2_, bf16[3,1024,1024]{2,1,0:T(8,128)(2,1)} %project_qkv.1.refs_0_.refs_1_.refs_2_, ...), custom_call_target="tpu_custom_call", output_to_operand_aliasing={{0}: (6, {})} | custom-call | flops 5368709120 | bytes 33849344 | tf_op jit(solution)/shard_map/attend_back/pallas_call | solution.py:212
  342.4 12.3 %grad_qkv.1 = (bf16[4,4,96,1024]{3,2,1,0:T(8,128)(2,1)}, bf16[4,4,96,1024]{3,2,1,0:T(8,128)(2,1)}) custom-call(s32[3]{0:T(128)} %pad_add_fusion.info_ref, bf16[1024,1024]{1,0:T(8,128)(2,1)} %refs_0_.7, bf16[3,1024,1024]{2,1,0:T(8,128)(2,1)} %get-tuple-element.314.refs_1_), custom_call_target="tpu_custom_call" | custom-call | flops 6442450944 | bytes 14680064 | tf_op jit(solution)/shard_map/grad_qkv/pallas_call | solution.py:212
  364.1 13.1 %input_back.1 = bf16[1024,1024]{1,0:T(8,128)(2,1)} custom-call(s32[3]{0:T(128)} %pad_add_fusion.info_ref, bf16[1024,1024]{1,0:T(8,128)(2,1)} %get-tuple-element.275.refs_3_.refs_0_, bf16[3,1024,1024]{2,1,0:T(8,128)(2,1)} %get-tuple-element.314.refs_1_, bf16[384,1024]{1,0:T(8,128)(2,1)} %copy-done.8, bf16[384,1024]{1,0:T(8,128)(2,1)} %copy-done.15, ...), custom_call_target="tpu_custom_call" | custom-call | flops 6442450944 | bytes 16777216 | tf_op jit(solution)/shard_map/input_back/pallas_call | solution.py:212
  402.0 9.2 %collective-permute-done.69 = bf16[4,96,1024]{2,1,0:T(8,128)(2,1)S(1)} collective-permute-done((bf16[4,96,1024]{2,1,0:T(8,128)(2,1)S(1)}, bf16[4,96,1024]{2,1,0:T(8,128)(2,1)S(1)}, u32[]{:S(2)}, u32[]{:S(2)}) %collective-permute-start.69) | collective-permute-done | bytes 786464 | tf_op jit(solution)/shard_map/ppermute | solution.py:52
  413.2 7.2 %collective-permute-done.77 = bf16[160,1024]{1,0:T(8,128)(2,1)S(1)} collective-permute-done((bf16[160,1024]{1,0:T(8,128)(2,1)S(1)}, bf16[160,1024]{1,0:T(8,128)(2,1)S(1)}, u32[]{:S(2)}, u32[]{:S(2)}) %collective-permute-start.77) | collective-permute-done | bytes 327712 | tf_op jit(solution)/shard_map/ppermute | solution.py:52
  427.9 6.8 %collective-permute-start.72 = (bf16[96,1024]{1,0:T(8,128)(2,1)S(1)}, bf16[96,1024]{1,0:T(8,128)(2,1)S(1)}, u32[]{:S(2)}, u32[]{:S(2)}) collective-permute-start(bf16[96,1024]{1,0:T(8,128)(2,1)S(1)} %get-tuple-element.354), channel_id=1, source_target_pairs={{0,16},{1,17},{2,18},{3,19},{4,20},{5,21},{6,22},{7,23},{8,24},{9,... | collective-permute-start | bytes 589832 | tf_op jit(solution)/shard_map/ppermute | solution.py:52
  437.7 11.2 %collective-permute-done.72 = bf16[96,1024]{1,0:T(8,128)(2,1)S(1)} collective-permute-done((bf16[96,1024]{1,0:T(8,128)(2,1)S(1)}, bf16[96,1024]{1,0:T(8,128)(2,1)S(1)}, u32[]{:S(2)}, u32[]{:S(2)}) %collective-permute-start.72) | collective-permute-done | bytes 196640 | tf_op jit(solution)/shard_map/ppermute | solution.py:52
  (277 shorter events, 154.2 us)
Async XLA Ops:
  25.2 20.7 %collective-permute-start.7 = (bf16[384,1024]{1,0:T(8,128)(2,1)S(1)}, bf16[384,1024]{1,0:T(8,128)(2,1)S(1)}, u32[]{:S(2)}, u32[]{:S(2)}) collective-permute-start(bf16[384,1024]{1,0:T(8,128)(2,1)S(1)} %pad_maximum_fusion.1.refs_2_), channel_id=1, source_target_pairs={{0,4},{1,5},{2,6},{3,7},{4,0},{5,1},{6,2},{7,3},{8,12},{9,13},{10,... | collective-permute-start | bytes 2359304 | tf_op jit(solution)/shard_map/ppermute | solution.py:52
  71.6 33.6 %collective-permute-start.25 = (bf16[640,1024]{1,0:T(8,128)(2,1)S(1)}, bf16[640,1024]{1,0:T(8,128)(2,1)S(1)}, u32[]{:S(2)}, u32[]{:S(2)}) collective-permute-start(bf16[640,1024]{1,0:T(8,128)(2,1)S(1)} %constant_dynamic-update-slice_fusion.refs_3_.refs_2_.refs_4_.refs_5_), channel_id=1, source_target_pairs={{0,4},{1,5},{2,6},{3,7},{4,0},{5,1},{6,2},{7,3},{8,12},{9,13},{10,... | collective-permute-start | bytes 3932168 | tf_op jit(solution)/shard_map/ppermute | solution.py:52
  73.1 32.1 %collective-permute-start.24 = (bf16[640,1024]{1,0:T(8,128)(2,1)S(1)}, bf16[640,1024]{1,0:T(8,128)(2,1)S(1)}, u32[]{:S(2)}, u32[]{:S(2)}) collective-permute-start(bf16[640,1024]{1,0:T(8,128)(2,1)S(1)} %constant_dynamic-update-slice_fusion.refs_3_.refs_2_.refs_4_.refs_5_), channel_id=1, source_target_pairs={{0,2},{1,3},{2,0},{3,1},{4,6},{5,7},{6,4},{7,5},{8,10},{9,11},{10,... | collective-permute-start | bytes 3932168 | tf_op jit(solution)/shard_map/ppermute | solution.py:52
  74.8 30.2 %collective-permute-start.28 = (bf16[128,1024]{1,0:T(8,128)(2,1)}, bf16[128,1024]{1,0:T(8,128)(2,1)}, u32[]{:S(2)}, u32[]{:S(2)}) collective-permute-start(bf16[128,1024]{1,0:T(8,128)(2,1)} %param.32), channel_id=1, source_target_pairs={{0,24},{1,25},{2,26},{3,27},{4,28},{5,29},{6,30},{7,31},{8,16},{9,... | collective-permute-start | bytes 786440 | tf_op jit(solution)/shard_map/ppermute | solution.py:52
  77.1 28.0 %collective-permute-start.27 = (bf16[128,1024]{1,0:T(8,128)(2,1)}, bf16[128,1024]{1,0:T(8,128)(2,1)}, u32[]{:S(2)}, u32[]{:S(2)}) collective-permute-start(bf16[128,1024]{1,0:T(8,128)(2,1)} %param.32), channel_id=1, source_target_pairs={{0,16},{1,17},{2,18},{3,19},{4,20},{5,21},{6,22},{7,23},{8,24},{9,... | collective-permute-start | bytes 786440 | tf_op jit(solution)/shard_map/ppermute | solution.py:52
  77.1 28.0 %collective-permute-start.26 = (bf16[128,1024]{1,0:T(8,128)(2,1)}, bf16[128,1024]{1,0:T(8,128)(2,1)}, u32[]{:S(2)}, u32[]{:S(2)}) collective-permute-start(bf16[128,1024]{1,0:T(8,128)(2,1)} %param.32), channel_id=1, source_target_pairs={{0,8},{1,9},{2,10},{3,11},{4,12},{5,13},{6,14},{7,15},{8,0},{9,1},... | collective-permute-start | bytes 786440 | tf_op jit(solution)/shard_map/ppermute | solution.py:52
  105.2 20.7 %collective-permute-start.32 = (bf16[640,1024]{1,0:T(8,128)(2,1)S(1)}, bf16[640,1024]{1,0:T(8,128)(2,1)}, u32[]{:S(2)}, u32[]{:S(2)}) collective-permute-start(bf16[640,1024]{1,0:T(8,128)(2,1)S(1)} %collective-permute-done.24.refs_4_.refs_3_.refs_5_.refs_6_), channel_id=1, source_target_pairs={{0,1},{1,0},{2,3},{3,2},{4,5},{5,4},{6,7},{7,6},{8,9},{9,8},{10,11... | collective-permute-start | bytes 3932168 | tf_op jit(solution)/shard_map/ppermute | solution.py:52
  126.4 28.0 %collective-permute-start.37 = (bf16[512,1024]{1,0:T(8,128)(2,1)}, bf16[512,1024]{1,0:T(8,128)(2,1)S(1)}, u32[]{:S(2)}, u32[]{:S(2)}) collective-permute-start(bf16[512,1024]{1,0:T(8,128)(2,1)} %pad_maximum_fusion.refs_4_.refs_2_), channel_id=1, source_target_pairs={{0,4},{1,5},{2,6},{3,7},{4,0},{5,1},{6,2},{7,3},{8,12},{9,13},{10,... | collective-permute-start | bytes 3145736 | tf_op jit(solution)/shard_map/ppermute | solution.py:52
  126.9 27.5 %collective-permute-start.36 = (bf16[512,1024]{1,0:T(8,128)(2,1)}, bf16[512,1024]{1,0:T(8,128)(2,1)}, u32[]{:S(2)}, u32[]{:S(2)}) collective-permute-start(bf16[512,1024]{1,0:T(8,128)(2,1)} %pad_maximum_fusion.refs_4_.refs_2_), channel_id=1, source_target_pairs={{0,2},{1,3},{2,0},{3,1},{4,6},{5,7},{6,4},{7,5},{8,10},{9,11},{10,... | collective-permute-start | bytes 3145736 | tf_op jit(solution)/shard_map/ppermute | solution.py:52
  237.4 24.6 %collective-permute-start.46 = (bf16[2,128,1024]{2,1,0:T(8,128)(2,1)}, bf16[2,128,1024]{2,1,0:T(8,128)(2,1)S(1)}, u32[]{:S(2)}, u32[]{:S(2)}) collective-permute-start(bf16[2,128,1024]{2,1,0:T(8,128)(2,1)} %get-tuple-element.263), channel_id=1, source_target_pairs={{0,2},{1,3},{2,0},{3,1},{4,6},{5,7},{6,4},{7,5},{8,10},{9,11},{10,... | collective-permute-start | bytes 1572872 | tf_op jit(solution)/shard_map/ppermute | solution.py:52
  238.4 23.6 %collective-permute-start.47 = (bf16[2,128,1024]{2,1,0:T(8,128)(2,1)S(1)}, bf16[2,128,1024]{2,1,0:T(8,128)(2,1)S(1)}, u32[]{:S(2)}, u32[]{:S(2)}) collective-permute-start(bf16[2,128,1024]{2,1,0:T(8,128)(2,1)S(1)} %get-tuple-element.264), channel_id=1, source_target_pairs={{0,4},{1,5},{2,6},{3,7},{4,0},{5,1},{6,2},{7,3},{8,12},{9,13},{10,... | collective-permute-start | bytes 1572872 | tf_op jit(solution)/shard_map/ppermute | solution.py:52
  238.9 24.2 %collective-permute-start.48 = (bf16[2,128,1024]{2,1,0:T(8,128)(2,1)S(1)}, bf16[2,128,1024]{2,1,0:T(8,128)(2,1)}, u32[]{:S(2)}, u32[]{:S(2)}) collective-permute-start(bf16[2,128,1024]{2,1,0:T(8,128)(2,1)S(1)} %get-tuple-element.265), channel_id=1, source_target_pairs={{0,2},{1,3},{2,0},{3,1},{4,6},{5,7},{6,4},{7,5},{8,10},{9,11},{10,... | collective-permute-start | bytes 1572872 | tf_op jit(solution)/shard_map/ppermute | solution.py:52
  239.8 23.8 %collective-permute-start.49 = (bf16[2,128,1024]{2,1,0:T(8,128)(2,1)S(1)}, bf16[2,128,1024]{2,1,0:T(8,128)(2,1)}, u32[]{:S(2)}, u32[]{:S(2)}) collective-permute-start(bf16[2,128,1024]{2,1,0:T(8,128)(2,1)S(1)} %get-tuple-element.266), channel_id=1, source_target_pairs={{0,4},{1,5},{2,6},{3,7},{4,0},{5,1},{6,2},{7,3},{8,12},{9,13},{10,... | collective-permute-start | bytes 1572872 | tf_op jit(solution)/shard_map/ppermute | solution.py:52
  284.5 27.9 %collective-permute-start.52 = (bf16[4,4,160,1024]{3,2,1,0:T(8,128)(2,1)}, bf16[4,4,160,1024]{3,2,1,0:T(8,128)(2,1)}, u32[]{:S(2)}, u32[]{:S(2)}) collective-permute-start(bf16[4,4,160,1024]{3,2,1,0:T(8,128)(2,1)} %get-tuple-element.279), channel_id=1, source_target_pairs={{0,1},{1,0},{2,3},{3,2},{4,5},{5,4},{6,7},{7,6},{8,9},{9,8},{10,11... | collective-permute-start | bytes 15728648 | tf_op jit(solution)/shard_map/ppermute | solution.py:52
  287.3 22.5 %collective-permute-start.55 = (bf16[128,1024]{1,0:T(8,128)(2,1)S(1)}, bf16[128,1024]{1,0:T(8,128)(2,1)S(1)}, u32[]{:S(2)}, u32[]{:S(2)}) collective-permute-start(bf16[128,1024]{1,0:T(8,128)(2,1)S(1)} %get-tuple-element.342), channel_id=1, source_target_pairs={{0,24},{1,25},{2,26},{3,27},{4,28},{5,29},{6,30},{7,31},{8,16},{9,... | collective-permute-start | bytes 786440 | tf_op jit(solution)/shard_map/ppermute | solution.py:52
  289.9 22.5 %collective-permute-start.54 = (bf16[128,1024]{1,0:T(8,128)(2,1)S(1)}, bf16[128,1024]{1,0:T(8,128)(2,1)S(1)}, u32[]{:S(2)}, u32[]{:S(2)}) collective-permute-start(bf16[128,1024]{1,0:T(8,128)(2,1)S(1)} %get-tuple-element.343), channel_id=1, source_target_pairs={{0,16},{1,17},{2,18},{3,19},{4,20},{5,21},{6,22},{7,23},{8,24},{9,... | collective-permute-start | bytes 786440 | tf_op jit(solution)/shard_map/ppermute | solution.py:52
  289.9 22.5 %collective-permute-start.53 = (bf16[128,1024]{1,0:T(8,128)(2,1)S(1)}, bf16[128,1024]{1,0:T(8,128)(2,1)S(1)}, u32[]{:S(2)}, u32[]{:S(2)}) collective-permute-start(bf16[128,1024]{1,0:T(8,128)(2,1)S(1)} %get-tuple-element.347), channel_id=1, source_target_pairs={{0,8},{1,9},{2,10},{3,11},{4,12},{5,13},{6,14},{7,15},{8,0},{9,1},... | collective-permute-start | bytes 786440 | tf_op jit(solution)/shard_map/ppermute | solution.py:52
  320.5 34.1 %collective-permute-start.56 = (bf16[2,160,1024]{2,1,0:T(8,128)(2,1)}, bf16[2,160,1024]{2,1,0:T(8,128)(2,1)}, u32[]{:S(2)}, u32[]{:S(2)}) collective-permute-start(bf16[2,160,1024]{2,1,0:T(8,128)(2,1)} %get-tuple-element.294), channel_id=1, source_target_pairs={{0,2},{1,3},{2,0},{3,1},{4,6},{5,7},{6,4},{7,5},{8,10},{9,11},{10,... | collective-permute-start | bytes 1966088 | tf_op jit(solution)/shard_map/ppermute | solution.py:52
  321.6 33.0 %collective-permute-start.57 = (bf16[2,160,1024]{2,1,0:T(8,128)(2,1)S(1)}, bf16[2,160,1024]{2,1,0:T(8,128)(2,1)}, u32[]{:S(2)}, u32[]{:S(2)}) collective-permute-start(bf16[2,160,1024]{2,1,0:T(8,128)(2,1)S(1)} %get-tuple-element.295), channel_id=1, source_target_pairs={{0,4},{1,5},{2,6},{3,7},{4,0},{5,1},{6,2},{7,3},{8,12},{9,13},{10,... | collective-permute-start | bytes 1966088 | tf_op jit(solution)/shard_map/ppermute | solution.py:52
  323.1 31.5 %collective-permute-start.58 = (bf16[2,160,1024]{2,1,0:T(8,128)(2,1)S(1)}, bf16[2,160,1024]{2,1,0:T(8,128)(2,1)}, u32[]{:S(2)}, u32[]{:S(2)}) collective-permute-start(bf16[2,160,1024]{2,1,0:T(8,128)(2,1)S(1)} %get-tuple-element.296), channel_id=1, source_target_pairs={{0,2},{1,3},{2,0},{3,1},{4,6},{5,7},{6,4},{7,5},{8,10},{9,11},{10,... | collective-permute-start | bytes 1966088 | tf_op jit(solution)/shard_map/ppermute | solution.py:52
  324.2 30.5 %collective-permute-start.59 = (bf16[2,160,1024]{2,1,0:T(8,128)(2,1)S(1)}, bf16[2,160,1024]{2,1,0:T(8,128)(2,1)}, u32[]{:S(2)}, u32[]{:S(2)}) collective-permute-start(bf16[2,160,1024]{2,1,0:T(8,128)(2,1)S(1)} %get-tuple-element.297), channel_id=1, source_target_pairs={{0,4},{1,5},{2,6},{3,7},{4,0},{5,1},{6,2},{7,3},{8,12},{9,13},{10,... | collective-permute-start | bytes 1966088 | tf_op jit(solution)/shard_map/ppermute | solution.py:52
  354.7 24.5 %collective-permute-start.60 = (bf16[4,4,96,1024]{3,2,1,0:T(8,128)(2,1)}, bf16[4,4,96,1024]{3,2,1,0:T(8,128)(2,1)}, u32[]{:S(2)}, u32[]{:S(2)}) collective-permute-start(bf16[4,4,96,1024]{3,2,1,0:T(8,128)(2,1)} %get-tuple-element.304), channel_id=1, source_target_pairs={{0,1},{1,0},{2,3},{3,2},{4,5},{5,4},{6,7},{7,6},{8,9},{9,8},{10,11... | collective-permute-start | bytes 9437192 | tf_op jit(solution)/shard_map/ppermute | solution.py:52
  398.5 21.9 %collective-permute-start.77 = (bf16[160,1024]{1,0:T(8,128)(2,1)S(1)}, bf16[160,1024]{1,0:T(8,128)(2,1)S(1)}, u32[]{:S(2)}, u32[]{:S(2)}) collective-permute-start(bf16[160,1024]{1,0:T(8,128)(2,1)S(1)} %get-tuple-element.333), channel_id=1, source_target_pairs={{0,16},{1,17},{2,18},{3,19},{4,20},{5,21},{6,22},{7,23},{8,24},{9,... | collective-permute-start | bytes 983048 | tf_op jit(solution)/shard_map/ppermute | solution.py:52
  427.9 21.0 %collective-permute-start.72 = (bf16[96,1024]{1,0:T(8,128)(2,1)S(1)}, bf16[96,1024]{1,0:T(8,128)(2,1)S(1)}, u32[]{:S(2)}, u32[]{:S(2)}) collective-permute-start(bf16[96,1024]{1,0:T(8,128)(2,1)S(1)} %get-tuple-element.354), channel_id=1, source_target_pairs={{0,16},{1,17},{2,18},{3,19},{4,20},{5,21},{6,22},{7,23},{8,24},{9,... | collective-permute-start | bytes 589832 | tf_op jit(solution)/shard_map/ppermute | solution.py:52
  (84 other events, 995.6 us)
